TPU v7x, 256 devices: a whole 4x4x8 slice. The times are simulated.
256 devices in a mesh: tm: 64 (over z, x, core), space: 4 (over y).
Axes of the slice: x: 4, y: 4, z: 8, core: 2. Of those that a mesh axis runs over, the one named last changes fastest.
Arguments:
- states: float32 [64, 2, 64, 256], P('tm', None, 'space'), may hold values from -6 to 6
- vel_x: int32 [64, 256], replicated, may hold values from -15 to 15
- vel_y: int32 [64, 256], replicated, may hold values from -15 to 15
- diffus: int32 [64, 256], replicated, may hold values from 1 to 10
Outputs:
- corrected: float32 [64, 2, 64, 256], P('tm', None, 'space')
- advanced: float32 [64, 2, 64, 256], P('tm', None, 'space')
- residual: float32 [64, 2, 64, 256], P('tm', None, 'space')
All inputs are finite; a program needn't handle non-finite values.
Results may differ from a plain program's by a relative error of at most 0.00002.
Values sent between devices are 32-bit elements; how exact they have to be, the bound alone decides.
No kernel may reach another device: no remote copies, remote signals or barrier semaphores. Data moves between devices by JAX's collectives and lax.ppermute only.
A program may use at most 64 MiB of HBM per device.

v0:
```python
import jax
import jax.numpy as jnp
from jax import lax
from jax.sharding import PartitionSpec as P

STEPS = 16


def extended_2(block, sides, width):
    for axis, dim in sides:
        count = lax.axis_size(axis)
        forward = [(i, i + 1) for i in range(count - 1)]
        backward = [(target, source) for source, target in forward]
        low = lax.ppermute(
            lax.slice_in_dim(block, block.shape[dim] - width, None, axis=dim), axis, forward
        )
        high = lax.ppermute(lax.slice_in_dim(block, 0, width, axis=dim), axis, backward)
        block = jnp.concatenate([low, block, high], axis=dim)
    return block


def from_behind(value, axis, steps):
    count = lax.axis_size(axis)
    initial, last = (max(0, -steps), min(count, count - steps))
    return lax.ppermute(value, axis, [(source, source + steps) for source in range(initial, last)])


def tracer_scales():
    return jnp.array([1.0, 0.5], jnp.float32)[:, None, None]


def coefficients(vel_x, vel_y, diffus):
    return (
        0.01 * vel_x.astype(jnp.float32),
        0.01 * vel_y.astype(jnp.float32),
        0.005 * diffus.astype(jnp.float32),
    )


def advance(field, coefs, factor):
    courant_x, courant_y, diffusion = coefs
    padded = jnp.pad(field, ((0, 0), (1, 1), (1, 1)))
    row_above = padded[:, :-2, 1:-1]
    row_below = padded[:, 2:, 1:-1]
    column_left = padded[:, 1:-1, :-2]
    column_right = padded[:, 1:-1, 2:]
    transport = (
        jnp.maximum(courant_x, 0.0) * (field - row_above)
        + jnp.minimum(courant_x, 0.0) * (row_below - field)
        + jnp.maximum(courant_y, 0.0) * (field - column_left)
        + jnp.minimum(courant_y, 0.0) * (column_right - field)
    )
    laplace = row_above + row_below + column_left + column_right - 4.0 * field
    return field + factor * (diffusion * tracer_scales() * laplace - transport)


def on_device(states, vel_x, vel_y, diffus):
    row_count = states.shape[2]
    fine_reach = 4
    coarse_reach = 8
    grid_rows = vel_x.shape[0]
    tile_index = lax.axis_index("space")
    full_coefs = coefficients(vel_x, vel_y, diffus)

    def window(coefficient_table, reach):
        padded = jnp.pad(coefficient_table, ((reach, reach), (0, 0)))
        return lax.dynamic_slice_in_dim(padded, tile_index * row_count, row_count + 2 * reach, 0)

    def inside_mask(reach):
        global_row = tile_index * row_count - reach + lax.iota(jnp.int32, row_count + 2 * reach)
        return ((global_row >= 0) & (global_row < grid_rows)).astype(jnp.float32)[:, None]

    fine_coefs = tuple((window(table, fine_reach) for table in full_coefs))
    fine_inside = inside_mask(fine_reach)
    coarse_coefs = tuple((window(table, coarse_reach) for table in full_coefs))
    coarse_inside = inside_mask(coarse_reach)

    def fine_steps(field):
        for block_index in range(STEPS // fine_reach):
            extended = extended_2(field, (("space", 1),), fine_reach)
            for inner_index in range(fine_reach):
                extended = advance(extended, fine_coefs, 1.0) * fine_inside
            field = extended[:, fine_reach : fine_reach + row_count]
        return field

    def coarse_block(block_index, current):
        extended = extended_2(current, (("space", 1),), coarse_reach)
        for inner_index in range(coarse_reach):
            extended = advance(extended, coarse_coefs, 2.0) * coarse_inside
        return extended[:, coarse_reach : coarse_reach + row_count]

    def coarse_steps(field, count):
        return lax.fori_loop(0, count // coarse_reach, coarse_block, field)

    initial = states[0]
    first_slot = lax.axis_index("tm") == 0
    interval_ends = fine_steps(initial)
    received = from_behind(interval_ends, "tm", 1)
    starts = jnp.where(first_slot, initial, received)
    second_ends = fine_steps(starts)
    coarse_starts = coarse_steps(starts, STEPS // 2)
    received_second, received_coarse = from_behind((second_ends, coarse_starts), "tm", 1)
    residual = jnp.where(first_slot, jnp.zeros_like(starts), received_second - starts)
    forcing = jnp.where(first_slot, initial, received_second - received_coarse)

    def sweep_turn(turn_index, carried):
        arrived = from_behind(carried, "tm", 1)
        return coarse_steps(arrived, STEPS // 2) + forcing

    corrected = lax.fori_loop(0, lax.axis_size("tm") - 1, sweep_turn, forcing)
    advanced = fine_steps(corrected)
    return (corrected[None], advanced[None], residual[None])


def solution(mesh):
    return jax.shard_map(
        on_device,
        mesh=mesh,
        in_specs=(P("tm", None, "space", None), P(), P(), P()),
        out_specs=(
            P("tm", None, "space", None),
            P("tm", None, "space", None),
            P("tm", None, "space", None),
        ),
        check_vma=False,
    )
```

profile of v0, /device:TPU:128, one launch (start us, length us, event | category | flops | bytes accessed | tf_op | source)
XLA Modules:
  0.0 1218.8 jit_solution(14868030897880391279)
XLA Ops:
  95.8 1090.5 %while.15 = (s32[]{:T(128)}, f32[2,16,256]{2,1,0:T(8,128)S(1)}, f32[32,256]{1,0:T(8,128)S(1)}, f32[32,256]{1,0:T(8,128)S(1)}, f32[32,256]{1,0:T(8,128)S(1)}, /*i...) while((s32[]{:T(128)}, f32[2,16,256]{2,1,0:T(8,128)S(1)}, ...), condition=%wide.region_1.2_spmd.clone.clone.clone, body=%wide.region_0.1_spmd.sunk.clone.clone.clone.sunk | while | flops 2834594 | bytes 3622353 | solution.py:110
  97.8 6.6 collective-permute-done
  115.5 6.6 collective-permute-done
  132.8 6.6 collective-permute-done
  150.1 6.6 collective-permute-done
  167.4 6.6 collective-permute-done
  184.7 6.6 collective-permute-done
  202.0 6.6 collective-permute-done
  219.3 6.6 collective-permute-done
  236.6 6.6 collective-permute-done
  253.9 6.6 collective-permute-done
  271.2 6.6 collective-permute-done
  288.5 6.6 collective-permute-done
  305.8 6.6 collective-permute-done
  323.1 6.6 collective-permute-done
  340.4 6.6 collective-permute-done
  357.7 6.6 collective-permute-done
  375.0 6.6 collective-permute-done
  392.3 6.6 collective-permute-done
  409.6 6.6 collective-permute-done
  426.9 6.6 collective-permute-done
  444.2 6.6 collective-permute-done
  461.5 6.6 collective-permute-done
  478.9 6.6 collective-permute-done
  496.2 6.6 collective-permute-done
  513.5 6.6 collective-permute-done
  530.8 6.6 collective-permute-done
  548.1 6.6 collective-permute-done
  565.4 6.6 collective-permute-done
  582.7 6.6 collective-permute-done
  600.0 6.6 collective-permute-done
  617.3 6.6 collective-permute-done
  634.6 6.6 collective-permute-done
  651.9 6.6 collective-permute-done
  669.2 6.6 collective-permute-done
  686.5 6.6 collective-permute-done
  703.8 6.6 collective-permute-done
  721.1 6.6 collective-permute-done
  738.4 6.6 collective-permute-done
  755.7 6.6 collective-permute-done
  773.0 6.6 collective-permute-done
  790.3 6.6 collective-permute-done
  807.6 6.6 collective-permute-done
  824.9 6.6 collective-permute-done
  842.2 6.6 collective-permute-done
  859.5 6.6 collective-permute-done
  876.8 6.6 collective-permute-done
  894.1 6.6 collective-permute-done
  911.4 6.6 collective-permute-done
  928.7 6.6 collective-permute-done
  946.0 6.6 collective-permute-done
  963.3 6.6 collective-permute-done
  980.6 6.6 collective-permute-done
  997.9 6.6 collective-permute-done
  1015.2 6.6 collective-permute-done
  1032.5 6.6 collective-permute-done
  1049.8 6.6 collective-permute-done
  1067.1 6.6 collective-permute-done
  1084.4 6.6 collective-permute-done
  1101.7 6.6 collective-permute-done
  1119.0 6.6 collective-permute-done
  1136.3 6.6 collective-permute-done
  1153.6 6.6 collective-permute-done
  1170.9 6.6 collective-permute-done
  (1573 shorter events, 793.8 us)
Async XLA Ops:
  38.0 8.5 collective-permute-start.11
  56.8 10.0 collective-permute-start.14
  61.0 12.3 %collective-permute-start.21 = (f32[2,8,256]{2,1,0:T(8,128)S(1)}, f32[2,8,256]{2,1,0:T(8,128)S(1)}, u32[]{:S(2)}, u32[]{:S(2)}) collective-permute-start(f32[2,8,256]{2,1,0:T(8,128)S(1)} %get-tuple-element.428), channel_id=1, source_target_pairs={{0,1},{1,2},{2,3},{4,5},{5,6},{6,7},{8,9},{9,10},{10,11},{12,13},{... | collective-permute-start | bytes 49160 | tf_op jit(solution)/shard_map/while/body/eval_jaxpr/ppermute | solution.py:14
  81.3 8.5 collective-permute-start.23
  86.0 8.5 collective-permute-start.20
  113.6 8.5 collective-permute-start
  130.9 8.5 collective-permute-start
  148.2 8.5 collective-permute-start
  165.5 8.5 collective-permute-start
  182.8 8.5 collective-permute-start
  200.1 8.5 collective-permute-start
  217.4 8.5 collective-permute-start
  234.7 8.5 collective-permute-start
  252.0 8.5 collective-permute-start
  269.3 8.5 collective-permute-start
  286.6 8.5 collective-permute-start
  303.9 8.5 collective-permute-start
  321.2 8.5 collective-permute-start
  338.5 8.5 collective-permute-start
  355.8 8.5 collective-permute-start
  373.1 8.5 collective-permute-start
  390.4 8.5 collective-permute-start
  407.7 8.5 collective-permute-start
  425.0 8.5 collective-permute-start
  442.3 8.5 collective-permute-start
  459.6 8.5 collective-permute-start
  476.9 8.5 collective-permute-start
  494.2 8.5 collective-permute-start
  511.5 8.5 collective-permute-start
  528.8 8.5 collective-permute-start
  546.1 8.5 collective-permute-start
  563.4 8.5 collective-permute-start
  580.7 8.5 collective-permute-start
  598.0 8.5 collective-permute-start
  615.3 8.5 collective-permute-start
  632.6 8.5 collective-permute-start
  649.9 8.5 collective-permute-start
  667.2 8.5 collective-permute-start
  684.5 8.5 collective-permute-start
  701.8 8.5 collective-permute-start
  719.1 8.5 collective-permute-start
  736.4 8.5 collective-permute-start
  753.7 8.5 collective-permute-start
  771.0 8.5 collective-permute-start
  788.4 8.5 collective-permute-start
  805.7 8.5 collective-permute-start
  823.0 8.5 collective-permute-start
  840.3 8.5 collective-permute-start
  857.6 8.5 collective-permute-start
  874.9 8.5 collective-permute-start
  892.2 8.5 collective-permute-start
  909.5 8.5 collective-permute-start
  926.8 8.5 collective-permute-start
  944.1 8.5 collective-permute-start
  961.4 8.5 collective-permute-start
  978.7 8.5 collective-permute-start
  996.0 8.5 collective-permute-start
  1013.3 8.5 collective-permute-start
  1030.6 8.5 collective-permute-start
  1047.9 8.5 collective-permute-start
  1065.2 8.5 collective-permute-start
  1082.5 8.5 collective-permute-start
  1099.8 8.5 collective-permute-start
  1151.7 8.5 collective-permute-start
  (162 other events, 793.2 us)
where the time goes:
time: 1230 us; the launch traced here: 1220 us
  waiting for transfers between devices  740 us (60%)
  starting transfers between devices  385 us (31%)
  other arithmetic  76.3 us (6%)
    ppermute x66, waiting for transfers between devices, from_behind(): lax.ppermute(value, axis, [(source, source + steps) for source in range(i...  429 us
    ppermute x76, waiting for transfers between devices, extended_2(): lax.ppermute(lax.slice_in_dim(block, 0, width, axis=dim), axis, backward)  307 us
    ppermute x76, starting transfers between devices, extended_2(): lax.ppermute(lax.slice_in_dim(block, block.shape[dim] - width, None, axis...  161 us
    ppermute x66, starting transfers between devices, from_behind(): lax.ppermute(value, axis, [(source, source + steps) for source in range(i...  126 us
    ppermute x76, starting transfers between devices, extended_2(): lax.ppermute(lax.slice_in_dim(block, 0, width, axis=dim), axis, backward)  97.5 us
    mul x385, other arithmetic, coarse_block(): extended = advance(extended, coarse_coefs, 2.0) * coarse_inside  45.9 us
  transfers between devices with their start and end apart: 218, of which 140 were waited for; matrix products, arithmetic and copies ran while one was open for 1% of the time, Pallas kernels for 0%

commit v1 on v0

v1 whole, which is shorter than its diff:
```python
import functools

import jax
import jax.numpy as jnp
import numpy as np
from jax import lax
from jax.experimental import pallas as pl
from jax.experimental.pallas import tpu as pltpu
from jax.sharding import Mesh
from jax.sharding import PartitionSpec as P

STEPS = 16
ROWS, COLS = 64, 256
PLANES, PLACES, PARTS = 8, 8, 4
INTERVALS = PLANES * PLACES
TILES = 16
VMEM = pl.BlockSpec(memory_space=pltpu.VMEM)
F32, BF16 = jnp.float32, jnp.bfloat16


def diamond(radius):
    reach = range(-radius, radius + 1)
    return [(dr, dc) for dr in reach for dc in reach if abs(dr) + abs(dc) <= radius]


class Shifted:
    def __init__(self, tiles):
        self.tiles, self.made = tiles, {}

    def at(self, i, column):
        lanes, j = divmod(column, 2)
        key = (i, j, lanes)
        if key not in self.made:
            if not 0 <= i < 8:
                self.made[key] = pltpu.roll(self.at(i % 8, column), 1 if i < 0 else 7, 0)
            elif lanes:
                self.made[key] = pltpu.roll(self.tiles[2 * i + j], (-lanes) % 128, 1)
            else:
                self.made[key] = self.tiles[2 * i + j]
        return self.made[key]


def apply(tiles, coef, radius):
    moved, points, result = Shifted(tiles), diamond(radius), []
    for i in range(8):
        for j in range(2):
            order = sorted(range(len(points)), key=lambda n: (abs((j + points[n][1]) // 2), points[n][1], points[n][0]))
            total = None
            for n in order:
                term = coef[n, 2 * i + j] * moved.at(i + points[n][0], j + points[n][1])
                total = term if total is None else total + term
            result.append(total)
    return tuple(result)


def five_point(levels, tracer, factor, out):
    lane = lax.broadcasted_iota(jnp.int32, (8, 128), 1)
    sublane = lax.broadcasted_iota(jnp.int32, (8, 128), 0)
    scale = jnp.where(tracer == 0, 1.0, 0.5).astype(F32)
    offsets = diamond(1)
    for i in range(8):
        for j in range(2):
            k = 2 * i + j
            courant_x, courant_y = 0.01 * levels[0, k], 0.01 * levels[1, k]
            spread = scale * (0.005 * levels[2, k])
            above = factor * (spread + jnp.maximum(courant_x, 0.0))
            below = factor * (spread - jnp.minimum(courant_x, 0.0))
            left = factor * (spread + jnp.maximum(courant_y, 0.0))
            right = factor * (spread - jnp.minimum(courant_y, 0.0))
            middle = 1.0 - factor * (4.0 * spread + jnp.abs(courant_x) + jnp.abs(courant_y))
            if i == 0:
                above = jnp.where(sublane == 0, 0.0, above)
            if i == 7:
                below = jnp.where(sublane == 7, 0.0, below)
            if j == 0:
                left = jnp.where(lane == 0, 0.0, left)
            if j == 1:
                right = jnp.where(lane == 127, 0.0, right)
            for offset, value in (((0, 0), middle), ((-1, 0), above), ((1, 0), below), ((0, -1), left), ((0, 1), right)):
                out[offsets.index(offset), k] = value


def compose(one, source, radius, out):
    near, old = diamond(1), diamond(radius)
    for n, (row, column) in enumerate(diamond(radius + 1)):
        totals = [None] * TILES
        for m, (dr, dc) in enumerate(near):
            if (row - dr, column - dc) not in old:
                continue
            at = old.index((row - dr, column - dc))
            moved = Shifted([source[at, k] for k in range(TILES)])
            for k in range(TILES):
                term = one[m, k] * moved.at(k // 2 + dr, k % 2 + dc)
                totals[k] = term if totals[k] is None else totals[k] + term
        for k in range(TILES):
            out[n, k] = totals[k]


def coef_scratch(radius):
    return pltpu.VMEM((len(diamond(radius)), TILES, 8, 128), F32)


def load_flat(ref, start=0):
    return tuple(ref[pl.ds(start + 2 * i + j, 8, stride=16), :] for i in range(8) for j in range(2))


def store_flat(ref, tiles):
    for i in range(8):
        for j in range(2):
            ref[pl.ds(2 * i + j, 8, stride=16), :] = tiles[2 * i + j]


def load_tiles(ref, *at):
    return tuple(ref[(*at, k)] for k in range(TILES))


def store_tiles(ref, tiles, *at):
    for k in range(TILES):
        ref[(*at, k)] = tiles[k]


def added(a, b):
    return tuple(x + y for x, y in zip(a, b, strict=True))


def split_matrix(back):
    row = lax.broadcasted_iota(jnp.int32, (COLS, COLS), 0)
    column = lax.broadcasted_iota(jnp.int32, (COLS, COLS), 1)
    if back:
        row, column = column, row
    return jnp.where(row == 2 * (column % 128) + column // 128, 1.0, 0.0).astype(BF16)


def permuted(x, matrix):
    high = x.astype(BF16)
    rest = x - high.astype(F32)
    middle = rest.astype(BF16)
    low = (rest - middle.astype(F32)).astype(BF16)
    dot = functools.partial(jnp.dot, preferred_element_type=F32)
    return (dot(high, matrix) + dot(middle, matrix)) + dot(low, matrix)


def prepare_kernel(states, out):
    both = jnp.concatenate([states[0, 0], states[0, 1]], 0)
    moved = permuted(both, split_matrix(False))
    for part in range(PARTS):
        rows = moved[16 * (part // 2) : 16 * (part // 2) + 16]
        for j in range(2):
            out[part, pl.ds(j, 16, stride=2), :] = rows[:, 128 * j : 128 * j + 128]


def own_kernel(whole, vel_x, vel_y, diffus, levels, carried, forcing, stage, fine1, coarse1, fine2, coarse2):
    interval = lax.axis_index("z") * PLACES + lax.axis_index("place")
    tracer = lax.axis_index("space") // 2
    matrix = split_matrix(False)
    for n, table in enumerate((vel_x, vel_y, diffus)):
        moved = jnp.dot(table[...].astype(F32).astype(BF16), matrix, preferred_element_type=F32)
        for j in range(2):
            stage[pl.ds(j, ROWS, stride=2), :] = moved[:, 128 * j : 128 * j + 128]
        store_tiles(levels, load_flat(stage), n)
    five_point(levels, tracer, 1.0, fine1)
    five_point(levels, tracer, 2.0, coarse1)
    compose(fine1, fine1, 1, fine2)
    compose(coarse1, coarse1, 1, coarse2)
    start = load_flat(whole)

    def body(_, fields):
        ahead, image = fields
        image = apply(image, coarse2, 2)
        ahead = apply(apply(ahead, fine2, 2), fine2, 2)
        return ahead, image

    ahead, image = lax.fori_loop(0, STEPS // 4, body, (start, start))
    store_tiles(carried, ahead)
    first = interval == 0
    for k in range(TILES):
        value = jnp.where(first, ahead[k], ahead[k] - image[k])
        for plane in range(PLANES):
            forcing[plane, k] = value


def coarse_interval(tiles, coarse2, coarse3):
    return apply(apply(apply(tiles, coarse3, 3), coarse3, 3), coarse2, 2)


def planes_kernel(forcings, levels, out, before, coarse1, coarse2, coarse3):
    plane, place = lax.axis_index("z"), lax.axis_index("place")
    tracer = lax.axis_index("space") // 2
    five_point(levels, tracer, 2.0, coarse1)
    compose(coarse1, coarse1, 1, coarse2)
    compose(coarse1, coarse2, 2, coarse3)
    store_tiles(before, tuple(jnp.zeros((8, 128), F32) for _ in range(TILES)))

    def one_plane(b, tiles):
        store_tiles(before, tiles)
        tiles = lax.fori_loop(0, PLACES, lambda _, now: coarse_interval(now, coarse2, coarse3), tiles)
        return added(tiles, load_tiles(forcings, b))

    total = lax.fori_loop(1, plane + 1, one_plane, load_tiles(forcings, 0))
    spare = (plane == PLANES - 1) & (place == 0)
    for target in range(PLACES):
        for k in range(TILES):
            value = jnp.where(place <= target, total[k], before[k])
            if target >= PLACES - 2:
                value = jnp.where(spare, forcings[0, k], value)
            out[target, k] = value


def finish_kernel(sums, following, carried, levels, out_a, out_b, corrected, left, stage, fine1, fine2, coarse1, coarse2, coarse3):
    plane, place, part = lax.axis_index("z"), lax.axis_index("place"), lax.axis_index("space")
    interval = plane * PLACES + place
    tracer = part // 2
    five_point(levels, tracer, 2.0, coarse1)
    compose(coarse1, coarse1, 1, coarse2)
    compose(coarse1, coarse2, 2, coarse3)
    five_point(levels, tracer, 1.0, fine1)
    compose(fine1, fine1, 1, fine2)

    def neighbour(k, tiles):
        at = lax.rem(place + 1 + k, PLACES)
        return added(coarse_interval(tiles, coarse2, coarse3), load_tiles(sums, at))

    total = lax.fori_loop(1, PLACES, neighbour, load_tiles(sums, lax.rem(place + 1, PLACES)))
    total = lax.fori_loop(0, STEPS // 2, lambda _, now: apply(now, fine2, 2), total)
    given = load_tiles(sums, 0)
    total = tuple(jnp.where(interval >= INTERVALS - 2, g, t) for g, t in zip(given, total, strict=True))
    store_tiles(corrected, total)
    gap = tuple(c - n for c, n in zip(load_tiles(carried), load_flat(following), strict=True))

    def body(_, fields):
        return tuple(apply(field, fine2, 2) for field in fields)

    advanced, residual = lax.fori_loop(0, STEPS // 2, body, (total, gap))
    advanced = tuple(jnp.where(interval == INTERVALS - 2, g, a) for g, a in zip(load_tiles(sums, 0), advanced, strict=True))
    to_a = 2 * lax.rem(part, 2) + part // 2
    to_b = 2 * lax.rem(part, 2) + 1 - part // 2
    for n, tiles in enumerate((load_tiles(corrected), advanced, residual)):
        store_flat(stage, tiles)
        out_a[pl.ds(32 * n, 32), :] = stage[pl.ds(pl.multiple_of(32 * to_a, 32), 32), :]
        out_b[pl.ds(32 * n, 32), :] = stage[pl.ds(pl.multiple_of(32 * to_b, 32), 32), :]


def assemble_kernel(got_a, got_b, states, corrected, advanced, residual):
    interval = lax.axis_index("z") * PLACES + lax.axis_index("place")
    odd = lax.rem(lax.axis_index("space"), 2)
    blocks = []
    for tracer in range(2):
        for n in range(3):
            halves = []
            for j in range(2):
                rows = pl.ds(32 * n + j, 16, stride=2)
                halves.append(jnp.where(odd == tracer, got_a[rows, :], got_b[rows, :]))
            blocks.append(jnp.concatenate(halves, 1))
    moved = permuted(jnp.concatenate(blocks, 0), split_matrix(True))
    for tracer in range(2):
        c, a, r = (moved[16 * (3 * tracer + n) : 16 * (3 * tracer + n) + 16] for n in range(3))
        corrected[0, tracer] = jnp.where(interval == 0, states[0, tracer], c)
        advanced[0, tracer] = a
        residual[0, tracer] = jnp.where(interval <= 1, 0.0, r)


def call(kernel, out_shapes, scratch, operands, flops):
    shapes = [jax.ShapeDtypeStruct(shape, F32) for shape in out_shapes]
    moved = 4 * sum(int(np.prod(shape)) for shape in list(out_shapes) + [x.shape for x in operands])
    return pl.pallas_call(
        kernel,
        out_shape=shapes,
        in_specs=[VMEM] * len(operands),
        out_specs=[VMEM] * len(shapes),
        scratch_shapes=scratch,
        compiler_params=pltpu.CompilerParams(vmem_limit_bytes=24 * 2**20),
        cost_estimate=pl.CostEstimate(flops=flops, bytes_accessed=moved, transcendentals=0),
    )(*operands)


def on_device(states, vel_x, vel_y, diffus):
    field = (TILES, 8, 128)
    (pieces,) = call(prepare_kernel, [(PARTS, 32, 128)], [], [states], 10**6)
    whole = lax.all_to_all(pieces, "space", 0, 0, tiled=True).reshape(128, 128)
    following = lax.ppermute(whole, ("z", "place"), [(i + 1, i) for i in range(INTERVALS - 1)])
    levels, carried, forcing = call(
        own_kernel,
        [(3, *field), field, (PLANES, *field)],
        [pltpu.VMEM((128, 128), F32), coef_scratch(1), coef_scratch(1), coef_scratch(2), coef_scratch(2)],
        [whole, vel_x, vel_y, diffus],
        10**7,
    )
    forcings = lax.all_to_all(forcing, "z", 0, 0, tiled=True)
    (sums,) = call(
        planes_kernel,
        [(PLACES, *field)],
        [pltpu.VMEM(field, F32), coef_scratch(1), coef_scratch(2), coef_scratch(3)],
        [forcings, levels],
        10**8,
    )
    sums = lax.all_to_all(sums, "place", 0, 0, tiled=True)
    to_a, to_b = call(
        finish_kernel,
        [(96, 128), (96, 128)],
        [pltpu.VMEM(field, F32), pltpu.VMEM(field, F32), pltpu.VMEM((128, 128), F32)]
        + [coef_scratch(1), coef_scratch(2), coef_scratch(1), coef_scratch(2), coef_scratch(3)],
        [sums, following, carried, levels],
        10**7,
    )
    axes = ("z", "place", "space")

    def route(place_of):
        return [
            (q * PARTS + part, (q + 2) % INTERVALS * PARTS + place_of(part))
            for q in range(INTERVALS)
            for part in range(PARTS)
        ]

    got_a = lax.ppermute(to_a, axes, route(lambda part: 2 * (part % 2) + part // 2))
    got_b = lax.ppermute(to_b, axes, route(lambda part: 2 * (part % 2) + 1 - part // 2))
    return tuple(call(assemble_kernel, [(1, 2, 16, COLS)] * 3, [], [got_a, got_b, states], 10**7))


def solution(mesh):
    grid = Mesh(mesh.devices.reshape(PLANES, PLACES, PARTS), ("z", "place", "space"))
    split = P(("z", "place"), None, "space", None)
    return jax.shard_map(
        on_device,
        mesh=grid,
        in_specs=(split, P(), P(), P()),
        out_specs=(split, split, split),
        check_vma=False,
    )
```

time: 1230 us -> 80.9 us (0.07)
  the two profiles are of different devices: /device:TPU:128 before, /device:TPU:1 now
where the time goes in v1:
time: 80.9 us; the launch traced here: 80.6 us
  blocking collectives  31.8 us (39%)
  waiting for transfers between devices  26.4 us (33%)
  starting transfers between devices  11.9 us (15%)
  Pallas kernels  8.99 us (11%)
    all_to_all x1, blocking collectives, on_device(): forcings = lax.all_to_all(forcing, 'z', 0, 0, tiled=True)  22.4 us
    ppermute x1, waiting for transfers between devices, on_device(): lax.ppermute(to_a, axes, route(lambda part: 2 * (part % 2) + part // 2))  17.8 us
    all_to_all x1, blocking collectives, on_device(): whole = lax.all_to_all(pieces, 'space', 0, 0, tiled=True).reshape(128, 128)  9.42 us
    pallas_call x5, Pallas kernels, call(): pl.pallas_call(kernel, out_shape=shapes, in_specs=[VMEM] * len(operands),...  8.99 us
    all_to_all x1, starting transfers between devices, on_device(): sums = lax.all_to_all(sums, 'place', 0, 0, tiled=True)  8.3 us
    ppermute x1, waiting for transfers between devices, on_device(): lax.ppermute(whole, ('z', 'place'), [(i + 1, i) for i in range(INTERVALS...  7.24 us
    ppermute x1, starting transfers between devices, on_device(): lax.ppermute(whole, ('z', 'place'), [(i + 1, i) for i in range(INTERVALS...  1.91 us
  transfers between devices with their start and end apart: 4, of which 4 were waited for; matrix products, arithmetic and copies ran while one was open for 0% of the time, Pallas kernels for 0%

profile of v1, /device:TPU:1, one launch (start us, length us, event | category | flops | bytes accessed | tf_op | source)
XLA Modules:
  0.0 80.6 jit_solution(5396032806072256469)
XLA Ops:
  0.6 0.0 copy-start
  0.6 0.7 copy-done
  1.4 0.0 copy-start.4
  1.4 0.2 shard_map.67
  1.6 0.0 copy-start.2
  1.6 0.0 copy-start.3
  1.6 9.4 %all_to_all.15 = f32[4,32,128]{2,1,0:T(8,128)S(1)} all-to-all(f32[4,32,128]{2,1,0:T(8,128)S(1)} %shard_map.67), channel_id=1, replica_groups=mesh['z'=8,'place'=8,'space'=4] {'space'}, dimensions={0} | all-to-all | bytes 131072 | tf_op jit(solution)/shard_map/all_to_all | solution.py:279
  11.0 0.0 copy-done.4
  11.0 0.0 copy-done.2
  11.0 0.0 copy-done.3
  11.0 1.5 %shard_map.68 = (f32[3,16,8,128]{3,2,1,0:T(8,128)S(1)}, f32[16,8,128]{2,1,0:T(8,128)S(1)}, f32[8,16,8,128]{3,2,1,0:T(8,128)S(1)}) custom-call(f32[128,128]{1,0:T(8,128)S(1)} %bitcast.1, s32[64,256]{1,0:T(8,128)S(1)} %copy-done.2, s32[64,256]{1,0:T(8,128)S(1)} %copy-done.3, s32[64,256]{1,0:T(8,128)S(1)} %copy-done.4), custom_call_target="tpu_custom_call" | custom-call | flops 10000000 | bytes 1048576 | tf_op jit(solution)/shard_map/pallas_call | solution.py:265
  12.6 22.4 %all_to_all.16.forcings = f32[8,16,8,128]{3,2,1,0:T(8,128)S(1)} all-to-all(f32[8,16,8,128]{3,2,1,0:T(8,128)S(1)} %get-tuple-element.8), channel_id=1, replica_groups=mesh['z'=8,'place'=8,'space'=4] {'z'}, dimensions={0} | all-to-all | bytes 1048576 | tf_op jit(solution)/shard_map/all_to_all | solution.py:288
  35.0 1.4 %shard_map.69 = f32[8,16,8,128]{3,2,1,0:T(8,128)} custom-call(f32[8,16,8,128]{3,2,1,0:T(8,128)S(1)} %all_to_all.16.forcings, f32[3,16,8,128]{3,2,1,0:T(8,128)S(1)} %get-tuple-element.9.levels), custom_call_target="tpu_custom_call" | custom-call | flops 100000000 | bytes 1245184 | tf_op jit(solution)/shard_map/pallas_call | solution.py:265
  36.4 8.3 %all-to-all-start.2 = ((f32[8,16,8,128]{3,2,1,0:T(8,128)}), f32[8,16,8,128]{3,2,1,0:T(8,128)S(1)}, u32[]{:S(2)}, u32[]{:S(2)}) async-start(f32[8,16,8,128]{3,2,1,0:T(8,128)} %shard_map.69), calls=%async_computation.2 | async-start | bytes 1048576 | tf_op jit(solution)/shard_map/all_to_all | solution.py:296
  44.7 1.9 %collective-permute-start = (f32[128,128]{1,0:T(8,128)S(1)}, f32[128,128]{1,0:T(8,128)S(1)}, u32[]{:S(2)}, u32[]{:S(2)}) collective-permute-start(f32[128,128]{1,0:T(8,128)S(1)} %bitcast.2), channel_id=1, source_target_pairs={{4,0},{8,4},{12,8},{16,12},{20,16},{24,20},{28,24},{32,28},{36,32}... | collective-permute-start | bytes 196616 | tf_op jit(solution)/shard_map/ppermute | solution.py:280
  46.6 7.2 %collective-permute-done.following = f32[128,128]{1,0:T(8,128)S(1)} collective-permute-done((f32[128,128]{1,0:T(8,128)S(1)}, f32[128,128]{1,0:T(8,128)S(1)}, u32[]{:S(2)}, u32[]{:S(2)}) %collective-permute-start) | collective-permute-done | bytes 65568 | tf_op jit(solution)/shard_map/ppermute | solution.py:280
  53.8 0.3 all-to-all-done.2.sums
  54.1 0.0 copy-start.1
  54.1 5.1 %shard_map.70 = (f32[96,128]{1,0:T(8,128)S(1)}, f32[96,128]{1,0:T(8,128)S(1)}) custom-call(f32[8,16,8,128]{3,2,1,0:T(8,128)S(1)} %all-to-all-done.2.sums, f32[128,128]{1,0:T(8,128)S(1)} %collective-permute-done.following, f32[16,8,128]{2,1,0:T(8,128)S(1)} %get-tuple-element.10.carried, f32[3,16,8,128]{3,2,1,0:T(8,128)S(1)} %get-tuple-element.9.levels), custom_call_target="tpu_custom_call" | custom-call | flops 10000000 | bytes 950272 | tf_op jit(solution)/shard_map/pallas_call | solution.py:265
  59.2 0.4 collective-permute-start.1
  59.6 1.3 %collective-permute-start.2 = (f32[96,128]{1,0:T(8,128)S(1)}, f32[96,128]{1,0:T(8,128)S(1)}, u32[]{:S(2)}, u32[]{:S(2)}) collective-permute-start(f32[96,128]{1,0:T(8,128)S(1)} %get-tuple-element.12), channel_id=1, source_target_pairs={{0,9},{1,11},{2,8},{3,10},{4,13},{5,15},{6,12},{7,14},{8,17},{9,19... | collective-permute-start | bytes 147464 | tf_op jit(solution)/shard_map/ppermute | solution.py:315
  60.9 17.8 %collective-permute-done.1.got_a = f32[96,128]{1,0:T(8,128)S(1)} collective-permute-done((f32[96,128]{1,0:T(8,128)S(1)}, f32[96,128]{1,0:T(8,128)S(1)}, u32[]{:S(2)}, u32[]{:S(2)}) %collective-permute-start.1) | collective-permute-done | bytes 49184 | tf_op jit(solution)/shard_map/ppermute | solution.py:314
  78.7 1.0 %collective-permute-done.2.got_b = f32[96,128]{1,0:T(8,128)S(1)} collective-permute-done((f32[96,128]{1,0:T(8,128)S(1)}, f32[96,128]{1,0:T(8,128)S(1)}, u32[]{:S(2)}, u32[]{:S(2)}) %collective-permute-start.2) | collective-permute-done | bytes 49184 | tf_op jit(solution)/shard_map/ppermute | solution.py:315
  79.7 0.0 copy-done.1
  79.7 0.8 %shard_map.71 = (f32[1,2,16,256]{3,2,1,0:T(8,128)}, f32[1,2,16,256]{3,2,1,0:T(8,128)}, f32[1,2,16,256]{3,2,1,0:T(8,128)}) custom-call(f32[96,128]{1,0:T(8,128)S(1)} %collective-permute-done.1.got_a, f32[96,128]{1,0:T(8,128)S(1)} %collective-permute-done.2.got_b, f32[1,2,16,256]{3,2,1,0:T(8,128)S(1)} %copy-done.1), custom_call_target="tpu_custom_call" | custom-call | flops 10000000 | bytes 229376 | tf_op jit(solution)/shard_map/pallas_call | solution.py:265
Async XLA Ops:
  0.6 0.8 copy-start
  1.4 9.6 %copy-start.4 = (s32[64,256]{1,0:T(8,128)S(1)}, s32[64,256]{1,0:T(8,128)}, u32[]{:S(2)}) copy-start(s32[64,256]{1,0:T(8,128)} %diffus.1) | copy-start | bytes 196612
  1.6 9.5 %copy-start.2 = (s32[64,256]{1,0:T(8,128)S(1)}, s32[64,256]{1,0:T(8,128)}, u32[]{:S(2)}) copy-start(s32[64,256]{1,0:T(8,128)} %vel_x.1) | copy-start | bytes 196612
  1.6 9.5 %copy-start.3 = (s32[64,256]{1,0:T(8,128)S(1)}, s32[64,256]{1,0:T(8,128)}, u32[]{:S(2)}) copy-start(s32[64,256]{1,0:T(8,128)} %vel_y.1) | copy-start | bytes 196612
  36.4 17.8 %all-to-all-start.2 = ((f32[8,16,8,128]{3,2,1,0:T(8,128)}), f32[8,16,8,128]{3,2,1,0:T(8,128)S(1)}, u32[]{:S(2)}, u32[]{:S(2)}) async-start(f32[8,16,8,128]{3,2,1,0:T(8,128)} %shard_map.69), calls=%async_computation.2 | async-start | bytes 1048576 | tf_op jit(solution)/shard_map/all_to_all | solution.py:296
  44.7 9.2 %collective-permute-start = (f32[128,128]{1,0:T(8,128)S(1)}, f32[128,128]{1,0:T(8,128)S(1)}, u32[]{:S(2)}, u32[]{:S(2)}) collective-permute-start(f32[128,128]{1,0:T(8,128)S(1)} %bitcast.2), channel_id=1, source_target_pairs={{4,0},{8,4},{12,8},{16,12},{20,16},{24,20},{28,24},{32,28},{36,32}... | collective-permute-start | bytes 196616 | tf_op jit(solution)/shard_map/ppermute | solution.py:280
  54.1 25.6 %copy-start.1 = (f32[1,2,16,256]{3,2,1,0:T(8,128)S(1)}, f32[1,2,16,256]{3,2,1,0:T(8,128)}, u32[]{:S(2)}) copy-start(f32[1,2,16,256]{3,2,1,0:T(8,128)} %states.3) | copy-start | bytes 98308
  59.2 19.5 %collective-permute-start.1 = (f32[96,128]{1,0:T(8,128)S(1)}, f32[96,128]{1,0:T(8,128)S(1)}, u32[]{:S(2)}, u32[]{:S(2)}) collective-permute-start(f32[96,128]{1,0:T(8,128)S(1)} %get-tuple-element.11), channel_id=1, source_target_pairs={{0,8},{1,10},{2,9},{3,11},{4,12},{5,14},{6,13},{7,15},{8,16},{9,18... | collective-permute-start | bytes 147464 | tf_op jit(solution)/shard_map/ppermute | solution.py:314
  59.6 20.1 %collective-permute-start.2 = (f32[96,128]{1,0:T(8,128)S(1)}, f32[96,128]{1,0:T(8,128)S(1)}, u32[]{:S(2)}, u32[]{:S(2)}) collective-permute-start(f32[96,128]{1,0:T(8,128)S(1)} %get-tuple-element.12), channel_id=1, source_target_pairs={{0,9},{1,11},{2,8},{3,10},{4,13},{5,15},{6,12},{7,14},{8,17},{9,19... | collective-permute-start | bytes 147464 | tf_op jit(solution)/shard_map/ppermute | solution.py:315

commit v2 on v1

v2 whole, which is shorter than its diff:
```python
import functools

import jax
import jax.numpy as jnp
import numpy as np
from jax import lax
from jax.experimental import pallas as pl
from jax.experimental.pallas import tpu as pltpu
from jax.sharding import Mesh
from jax.sharding import PartitionSpec as P

STEPS = 16
ROWS, COLS = 64, 256
PLANES, PLACES, PARTS = 8, 8, 4
INTERVALS = PLANES * PLACES
TILES = 16
VMEM = pl.BlockSpec(memory_space=pltpu.VMEM)
F32, BF16 = jnp.float32, jnp.bfloat16


def diamond(radius):
    reach = range(-radius, radius + 1)
    return [(dr, dc) for dr in reach for dc in reach if abs(dr) + abs(dc) <= radius]


class Shifted:
    def __init__(self, tiles):
        self.tiles, self.made = tiles, {}

    def at(self, i, column):
        lanes, j = divmod(column, 2)
        key = (i, j, lanes)
        if key not in self.made:
            if not 0 <= i < 8:
                self.made[key] = pltpu.roll(self.at(i % 8, column), 1 if i < 0 else 7, 0)
            elif lanes:
                self.made[key] = pltpu.roll(self.tiles[2 * i + j], (-lanes) % 128, 1)
            else:
                self.made[key] = self.tiles[2 * i + j]
        return self.made[key]


def apply(tiles, coef, radius):
    moved, points, result = Shifted(tiles), diamond(radius), []
    for i in range(8):
        for j in range(2):
            order = sorted(range(len(points)), key=lambda n: (abs((j + points[n][1]) // 2), points[n][1], points[n][0]))
            total = None
            for n in order:
                term = coef[n, 2 * i + j] * moved.at(i + points[n][0], j + points[n][1])
                total = term if total is None else total + term
            result.append(total)
    return tuple(result)


def five_point(levels, tracer, factor, out):
    lane = lax.broadcasted_iota(jnp.int32, (8, 128), 1)
    sublane = lax.broadcasted_iota(jnp.int32, (8, 128), 0)
    scale = jnp.where(tracer == 0, 1.0, 0.5).astype(F32)
    offsets = diamond(1)
    for i in range(8):
        for j in range(2):
            k = 2 * i + j
            courant_x, courant_y = 0.01 * levels[0, k], 0.01 * levels[1, k]
            spread = scale * (0.005 * levels[2, k])
            above = factor * (spread + jnp.maximum(courant_x, 0.0))
            below = factor * (spread - jnp.minimum(courant_x, 0.0))
            left = factor * (spread + jnp.maximum(courant_y, 0.0))
            right = factor * (spread - jnp.minimum(courant_y, 0.0))
            middle = 1.0 - factor * (4.0 * spread + jnp.abs(courant_x) + jnp.abs(courant_y))
            if i == 0:
                above = jnp.where(sublane == 0, 0.0, above)
            if i == 7:
                below = jnp.where(sublane == 7, 0.0, below)
            if j == 0:
                left = jnp.where(lane == 0, 0.0, left)
            if j == 1:
                right = jnp.where(lane == 127, 0.0, right)
            for offset, value in (((0, 0), middle), ((-1, 0), above), ((1, 0), below), ((0, -1), left), ((0, 1), right)):
                out[offsets.index(offset), k] = value


def compose(one, source, radius, out):
    near, old = diamond(1), diamond(radius)
    for n, (row, column) in enumerate(diamond(radius + 1)):
        totals = [None] * TILES
        for m, (dr, dc) in enumerate(near):
            if (row - dr, column - dc) not in old:
                continue
            at = old.index((row - dr, column - dc))
            moved = Shifted([source[at, k] for k in range(TILES)])
            for k in range(TILES):
                term = one[m, k] * moved.at(k // 2 + dr, k % 2 + dc)
                totals[k] = term if totals[k] is None else totals[k] + term
        for k in range(TILES):
            out[n, k] = totals[k]


def coef_scratch(radius):
    return pltpu.VMEM((len(diamond(radius)), TILES, 8, 128), F32)


def load_flat(ref, start=0):
    return tuple(ref[pl.ds(start + 2 * i + j, 8, stride=16), :] for i in range(8) for j in range(2))


def store_flat(ref, tiles):
    for i in range(8):
        for j in range(2):
            ref[pl.ds(2 * i + j, 8, stride=16), :] = tiles[2 * i + j]


def load_tiles(ref, *at):
    return tuple(ref[(*at, k)] for k in range(TILES))


def store_tiles(ref, tiles, *at):
    for k in range(TILES):
        ref[(*at, k)] = tiles[k]


def added(a, b):
    return tuple(x + y for x, y in zip(a, b, strict=True))


def split_matrix(back):
    row = lax.broadcasted_iota(jnp.int32, (COLS, COLS), 0)
    column = lax.broadcasted_iota(jnp.int32, (COLS, COLS), 1)
    if back:
        row, column = column, row
    return jnp.where(row == 2 * (column % 128) + column // 128, 1.0, 0.0).astype(BF16)


def permuted(x, matrix):
    high = x.astype(BF16)
    rest = x - high.astype(F32)
    middle = rest.astype(BF16)
    low = (rest - middle.astype(F32)).astype(BF16)
    dot = functools.partial(jnp.dot, preferred_element_type=F32)
    return (dot(high, matrix) + dot(middle, matrix)) + dot(low, matrix)


def prepare_kernel(states, out):
    both = jnp.concatenate([states[0, 0], states[0, 1]], 0)
    moved = permuted(both, split_matrix(False))
    for part in range(PARTS):
        rows = moved[16 * (part % 2) : 16 * (part % 2) + 16]
        for j in range(2):
            out[part, pl.ds(j, 16, stride=2), :] = rows[:, 128 * j : 128 * j + 128]


def read_levels(tables, levels, stage):
    matrix = split_matrix(False)
    for n, table in enumerate(range(3)):
        moved = jnp.dot(tables[table].astype(F32).astype(BF16), matrix, preferred_element_type=F32)
        for j in range(2):
            stage[pl.ds(j, ROWS, stride=2), :] = moved[:, 128 * j : 128 * j + 128]
        store_tiles(levels, load_flat(stage), n)


def steps_of(levels, factor, out):
    five_point(levels, lax.rem(lax.axis_index("space"), 2), factor, out[0])
    for n in range(len(out) - 1):
        compose(out[0], out[n], n + 1, out[n + 1])


def fine_interval(fields, fine2):
    return lax.fori_loop(0, STEPS // 2, lambda _, now: tuple(apply(field, fine2, 2) for field in now), fields)


def coarse_steps(tiles, count, coarse, planes):
    turns = jnp.where(lax.axis_index("z") >= planes, count // 3, 0)
    tiles = lax.fori_loop(0, turns, lambda _, now: apply(now, coarse[2], 3), tiles)
    return apply(tiles, coarse[count % 3 - 1], count % 3) if count % 3 else tiles


def coarse_interval(tiles, coarse):
    return apply(apply(apply(tiles, coarse[2], 3), coarse[2], 3), coarse[1], 2)


def where_me():
    return lax.axis_index("z") * PLACES + lax.axis_index("place")


def force(tiles, first, fine2, coarse):
    def body(_, fields):
        ahead, image = fields
        return apply(apply(ahead, fine2, 2), fine2, 2), apply(image, coarse[1], 2)

    ahead, image = lax.fori_loop(0, STEPS // 4, body, (tiles, tiles))
    return ahead, tuple(jnp.where(first, a, a - i) for a, i in zip(ahead, image, strict=True))


def own_kernel(whole, tables, fine2, coarse1, coarse2, coarse3, carried, forcing, stage, levels, fine1):
    read_levels(tables, levels, stage)
    steps_of(levels, 1.0, (fine1, fine2))
    steps_of(levels, 2.0, (coarse1, coarse2, coarse3))
    ahead, forced = force(load_flat(whole), where_me() == 0, fine2, (coarse1, coarse2))
    store_tiles(carried, ahead)
    store_tiles(forcing, forced)


def pair_kernel(behind, forcing, fine2, coarse1, coarse2, coarse3, before, pair):
    coarse = (coarse1, coarse2, coarse3)
    _, forced = force(load_flat(behind), where_me() == PLACES, fine2, coarse)
    store_tiles(before, forced)
    store_tiles(pair, added(coarse_steps(forced, 64, coarse, 1), load_tiles(forcing)))


def far_kernel(sixth, coarse1, coarse2, coarse3, out):
    store_tiles(out, coarse_steps(load_tiles(sixth), 128, (coarse1, coarse2, coarse3), 6))


def near_kernel(far, fourth, coarse1, coarse2, coarse3, out):
    total = added(load_tiles(far), load_tiles(fourth))
    store_tiles(out, coarse_steps(total, 128, (coarse1, coarse2, coarse3), 4))


def planes_kernel(near, second, before, forcing, whole, last, ahead, coarse1, coarse2, coarse3, out, gap, past, earlier):
    place, coarse = lax.axis_index("place"), (coarse1, coarse2, coarse3)
    total = added(load_tiles(near), load_tiles(second))
    store_tiles(earlier, total)
    total = added(coarse_steps(total, 64, coarse, 2), load_tiles(before))
    store_tiles(past, total)
    total = added(coarse_steps(total, 64, coarse, 1), load_tiles(forcing))
    store_tiles(gap, tuple(a - b for a, b in zip(load_tiles(ahead), load_flat(last), strict=True)))
    start = load_flat(whole)
    for target in range(PLACES):
        for k in range(TILES):
            value = jnp.where(place <= target - 2, total[k], past[k])
            if target == 0:
                value = jnp.where(place == PLACES - 1, earlier[k], value)
            if target == 1:
                value = jnp.where(where_me() == 0, start[k], value)
            out[target, k] = value


def finish_kernel(sums, gap, carried, fine2, coarse2, coarse3, give, keep, corrected, stage):
    place, part, me = lax.axis_index("place"), lax.axis_index("space"), where_me()
    coarse = (None, coarse2, coarse3)

    def neighbour(k, tiles):
        return added(coarse_interval(tiles, coarse), load_tiles(sums, lax.rem(place + 7 + k, PLACES)))

    total = lax.fori_loop(1, PLACES, neighbour, load_tiles(sums, lax.rem(place + 7, PLACES)))
    total = tuple(jnp.where(me == 1, sums[0, k], t) for k, t in enumerate(total))
    (total,) = fine_interval((total,), fine2)
    store_tiles(corrected, total)
    advanced, residual = fine_interval((total, load_tiles(gap)), fine2)
    advanced = tuple(jnp.where(me == 0, c, a) for c, a in zip(load_tiles(carried), advanced, strict=True))
    other = part + 1 - 2 * lax.rem(part, 2)
    for n, tiles in enumerate((load_tiles(corrected), advanced, residual)):
        store_flat(stage, tiles)
        give[pl.ds(32 * n, 32), :] = stage[pl.ds(pl.multiple_of(32 * other, 32), 32), :]
        keep[pl.ds(32 * n, 32), :] = stage[pl.ds(pl.multiple_of(32 * part, 32), 32), :]


def assemble_kernel(got, kept, states, corrected, advanced, residual):
    interval, own = where_me(), lax.rem(lax.axis_index("space"), 2)
    blocks = []
    for tracer in range(2):
        for n in range(3):
            halves = []
            for j in range(2):
                rows = pl.ds(32 * n + j, 16, stride=2)
                halves.append(jnp.where(own == tracer, kept[rows, :], got[rows, :]))
            blocks.append(jnp.concatenate(halves, 1))
    moved = permuted(jnp.concatenate(blocks, 0), split_matrix(True))
    for tracer in range(2):
        c, a, r = (moved[16 * (3 * tracer + n) : 16 * (3 * tracer + n) + 16] for n in range(3))
        corrected[0, tracer] = jnp.where(interval == 0, states[0, tracer], c)
        advanced[0, tracer] = a
        residual[0, tracer] = jnp.where(interval <= 1, 0.0, r)


def call(kernel, out_shapes, scratch, operands, flops):
    shapes = [jax.ShapeDtypeStruct(shape, F32) for shape in out_shapes]
    moved = 4 * sum(int(np.prod(x.shape)) for x in [*shapes, *operands])
    return pl.pallas_call(
        kernel,
        out_shape=shapes,
        in_specs=[VMEM] * len(operands),
        out_specs=[VMEM] * len(shapes),
        scratch_shapes=scratch,
        compiler_params=pltpu.CompilerParams(vmem_limit_bytes=24 * 2**20),
        cost_estimate=pl.CostEstimate(flops=flops, bytes_accessed=moved, transcendentals=0),
    )(*operands)


def on_device(states, vel_x, vel_y, diffus):
    field, axes = (TILES, 8, 128), ("z", "place")

    def onward(value, steps):
        return lax.ppermute(value, axes, [(i, i + steps) for i in range(INTERVALS - steps)])

    (pieces,) = call(prepare_kernel, [(PARTS, 32, 128)], [], [states], 10**6)
    whole = lax.all_to_all(pieces, "space", 0, 0, tiled=True).reshape(128, 128)
    behind = onward(whole, PLACES)
    stage = pltpu.VMEM((128, 128), F32)
    fine2, coarse1, coarse2, coarse3, carried, forcing = call(
        own_kernel,
        [(len(diamond(radius)), *field) for radius in (2, 1, 2, 3)] + [field, field],
        [stage, pltpu.VMEM((3, *field), F32), coef_scratch(1)],
        [whole, jnp.stack([vel_x, vel_y, diffus])],
        10**7,
    )
    coarse = [coarse1, coarse2, coarse3]
    before, pair = call(pair_kernel, [field, field], [], [behind, forcing, fine2, *coarse], 3 * 10**7)
    sixth, fourth, second = (onward(pair, planes * PLACES) for planes in (6, 4, 2))
    last, ahead = onward(whole, 1), onward(carried, 2)
    (far,) = call(far_kernel, [field], [], [sixth, *coarse], 5 * 10**7)
    (near,) = call(near_kernel, [field], [], [far, fourth, *coarse], 5 * 10**7)
    sums, gap = call(
        planes_kernel,
        [(PLACES, *field), field],
        [pltpu.VMEM(field, F32), pltpu.VMEM(field, F32)],
        [near, second, before, forcing, whole, last, ahead, *coarse],
        5 * 10**7,
    )
    sums = lax.all_to_all(sums, "place", 0, 0, tiled=True)
    give, keep = call(
        finish_kernel,
        [(96, 128), (96, 128)],
        [pltpu.VMEM(field, F32), stage],
        [sums, gap, carried, fine2, coarse2, coarse3],
        3 * 10**7,
    )
    got = lax.ppermute(give, "space", [(part, part ^ 1) for part in range(PARTS)])
    return tuple(call(assemble_kernel, [(1, 2, 16, COLS)] * 3, [], [got, keep, states], 10**7))


def solution(mesh):
    grid = Mesh(mesh.devices.reshape(PLANES, PLACES, PARTS), ("z", "place", "space"))
    split = P(("z", "place"), None, "space", None)
    return jax.shard_map(
        on_device,
        mesh=grid,
        in_specs=(split, P(), P(), P()),
        out_specs=(split, split, split),
        check_vma=False,
    )
```

time: 80.9 us -> 72.8 us (0.90)
  the two profiles are of different devices: /device:TPU:1 before, /device:TPU:64 now
where the time goes in v2:
time: 72.8 us; the launch traced here: 72.4 us
  blocking collectives  24.3 us (33%)
  starting transfers between devices  19.9 us (27%)
  Pallas kernels  17 us (23%)
  waiting for transfers between devices  8.85 us (12%)
  other arithmetic  0.92 us (1%)
  local copies, waits for them, and re-layouts  0.76 us (1%)
  between operations  0.76 us (1%)
    ppermute x6, starting transfers between devices, onward(): lax.ppermute(value, axes, [(i, i + steps) for i in range(INTERVALS - step...  19.2 us
    pallas_call x8, Pallas kernels, call(): pl.pallas_call(kernel, out_shape=shapes, in_specs=[VMEM] * len(operands),...  17 us
    all_to_all x1, blocking collectives, on_device(): sums = lax.all_to_all(sums, 'place', 0, 0, tiled=True)  14.3 us
    all_to_all x1, blocking collectives, on_device(): whole = lax.all_to_all(pieces, 'space', 0, 0, tiled=True).reshape(128, 128)  9.92 us
    ppermute x6, waiting for transfers between devices, onward(): lax.ppermute(value, axes, [(i, i + steps) for i in range(INTERVALS - step...  5.33 us
    ppermute x1, waiting for transfers between devices, on_device(): lax.ppermute(give, 'space', [(part, part ^ 1) for part in range(PARTS)])  3.53 us
  transfers between devices with their start and end apart: 7, of which 4 were waited for; matrix products, arithmetic and copies ran while one was open for 1% of the time, Pallas kernels for 3%

profile of v2, /device:TPU:64, one launch (start us, length us, event | category | flops | bytes accessed | tf_op | source)
XLA Modules:
  0.0 72.4 jit_solution(5769179371945936087)
XLA Ops:
  0.6 0.0 copy-start
  0.6 0.7 %copy-done = f32[1,2,16,256]{3,2,1,0:T(8,128)S(1)} copy-done((f32[1,2,16,256]{3,2,1,0:T(8,128)S(1)}, f32[1,2,16,256]{3,2,1,0:T(8,128)}, u32[]{:S(2)}) %copy-start) | copy-done | bytes 32792
  1.4 0.2 shard_map.67
  1.6 9.9 %all_to_all.10 = f32[4,32,128]{2,1,0:T(8,128)S(1)} all-to-all(f32[4,32,128]{2,1,0:T(8,128)S(1)} %shard_map.67), channel_id=1, replica_groups=mesh['z'=8,'place'=8,'space'=4] {'space'}, dimensions={0} | all-to-all | bytes 131072 | tf_op jit(solution)/shard_map/all_to_all | solution.py:297
  11.5 3.8 %collective-permute-start = (f32[128,128]{1,0:T(8,128)S(1)}, f32[128,128]{1,0:T(8,128)S(1)}, u32[]{:S(2)}, u32[]{:S(2)}) collective-permute-start(f32[128,128]{1,0:T(8,128)S(1)} %bitcast.4), channel_id=1, source_target_pairs={{0,32},{4,36},{8,40},{12,44},{16,48},{20,52},{24,56},{28,60},{32,6... | collective-permute-start | bytes 196616 | tf_op jit(solution)/shard_map/ppermute | solution.py:294
  15.3 0.9 %pad_add_fusion.tables = s32[3,64,256]{2,1,0:T(8,128)S(1)} fusion(s32[1,64,256]{2,1,0:T(8,128)} %bitcast.8, s32[1,64,256]{2,1,0:T(8,128)} %bitcast.9, s32[1,64,256]{2,1,0:T(8,128)} %bitcast.10), kind=kLoop, calls=%fused_computation | loop fusion | flops 98304 | bytes 393216 | tf_op jit(solution)/shard_map/stack | solution.py:304
  16.2 1.8 %shard_map.68 = (f32[13,16,8,128]{3,2,1,0:T(8,128)S(1)}, f32[5,16,8,128]{3,2,1,0:T(8,128)S(1)}, f32[13,16,8,128]{3,2,1,0:T(8,128)S(1)}, f32[25,16,8,128]{3,2,1,0...) custom-call(f32[128,128]{1,0:T(8,128)S(1)} %bitcast.5, s32[3,64,256]{2,1,0:T(8,128)S(1)} %pad_add_fusion.tables), custom_call_target="tpu_custom_call" | custom-call | flops 10000000 | bytes 4063232 | tf_op jit(solution)/shard_map/pallas_call | solution.py:279
  18.0 0.0 collective-permute-done.behind
  18.0 3.8 %shard_map.69 = (f32[16,8,128]{2,1,0:T(8,128)S(1)}, f32[16,8,128]{2,1,0:T(8,128)S(1)}) custom-call(f32[128,128]{1,0:T(8,128)S(1)} %collective-permute-done.behind, f32[16,8,128]{2,1,0:T(8,128)S(1)} %get-tuple-element.15.forcing, f32[13,16,8,128]{3,2,1,0:T(8,128)S(1)} %get-tuple-element.16.fine2, f32[5,16,8,128]{3,2,1,0:T(8,128)S(1)} %get-tuple-element.17.coarse1, ...), custom_call_target="tpu_custom_call" | custom-call | flops 30000000 | bytes 3932160 | tf_op jit(solution)/shard_map/pallas_call | solution.py:279
  21.8 0.7 collective-permute-start.1
  22.5 7.5 %collective-permute-start.2 = (f32[16,8,128]{2,1,0:T(8,128)S(1)}, f32[16,8,128]{2,1,0:T(8,128)S(1)}, u32[]{:S(2)}, u32[]{:S(2)}) collective-permute-start(f32[16,8,128]{2,1,0:T(8,128)S(1)} %get-tuple-element.20), channel_id=1, source_target_pairs={{0,128},{4,132},{8,136},{12,140},{16,144},{20,148},{24,152},{28,15... | collective-permute-start | bytes 196616 | tf_op jit(solution)/shard_map/ppermute | solution.py:294
  30.0 1.9 %collective-permute-start.4 = (f32[128,128]{1,0:T(8,128)S(1)}, f32[128,128]{1,0:T(8,128)S(1)}, u32[]{:S(2)}, u32[]{:S(2)}) collective-permute-start(f32[128,128]{1,0:T(8,128)S(1)} %bitcast.6), channel_id=1, source_target_pairs={{0,4},{4,8},{8,12},{12,16},{16,20},{20,24},{24,28},{28,32},{32,36}... | collective-permute-start | bytes 196616 | tf_op jit(solution)/shard_map/ppermute | solution.py:294
  32.0 3.4 %collective-permute-start.5 = (f32[16,8,128]{2,1,0:T(8,128)S(1)}, f32[16,8,128]{2,1,0:T(8,128)S(1)}, u32[]{:S(2)}, u32[]{:S(2)}) collective-permute-start(f32[16,8,128]{2,1,0:T(8,128)S(1)} %get-tuple-element.22.carried), channel_id=1, source_target_pairs={{0,8},{4,12},{8,16},{12,20},{16,24},{20,28},{24,32},{28,36},{32,40... | collective-permute-start | bytes 196616 | tf_op jit(solution)/shard_map/ppermute | solution.py:294
  35.4 1.9 %collective-permute-start.3 = (f32[16,8,128]{2,1,0:T(8,128)S(1)}, f32[16,8,128]{2,1,0:T(8,128)S(1)}, u32[]{:S(2)}, u32[]{:S(2)}) collective-permute-start(f32[16,8,128]{2,1,0:T(8,128)S(1)} %get-tuple-element.20), channel_id=1, source_target_pairs={{0,64},{4,68},{8,72},{12,76},{16,80},{20,84},{24,88},{28,92},{32,9... | collective-permute-start | bytes 196616 | tf_op jit(solution)/shard_map/ppermute | solution.py:294
  37.3 0.0 collective-permute-done.1.sixth
  37.3 0.1 shard_map.70.far
  37.4 0.0 collective-permute-done.2.fourth
  37.4 0.1 shard_map.71.near
  37.6 0.2 collective-permute-done.4.last
  37.7 2.6 %collective-permute-done.5.ahead = f32[16,8,128]{2,1,0:T(8,128)S(1)} collective-permute-done((f32[16,8,128]{2,1,0:T(8,128)S(1)}, f32[16,8,128]{2,1,0:T(8,128)S(1)}, u32[]{:S(2)}, u32[]{:S(2)}) %collective-permute-start.5) | collective-permute-done | bytes 65568 | tf_op jit(solution)/shard_map/ppermute | solution.py:294
  40.4 2.5 %collective-permute-done.3.second = f32[16,8,128]{2,1,0:T(8,128)S(1)} collective-permute-done((f32[16,8,128]{2,1,0:T(8,128)S(1)}, f32[16,8,128]{2,1,0:T(8,128)S(1)}, u32[]{:S(2)}, u32[]{:S(2)}) %collective-permute-start.3) | collective-permute-done | bytes 65568 | tf_op jit(solution)/shard_map/ppermute | solution.py:294
  42.9 5.8 %shard_map.72 = (f32[8,16,8,128]{3,2,1,0:T(8,128)S(1)}, f32[16,8,128]{2,1,0:T(8,128)S(1)}) custom-call(f32[16,8,128]{2,1,0:T(8,128)S(1)} %shard_map.71.near, f32[16,8,128]{2,1,0:T(8,128)S(1)} %collective-permute-done.3.second, f32[16,8,128]{2,1,0:T(8,128)S(1)} %get-tuple-element.21.before, f32[16,8,128]{2,1,0:T(8,128)S(1)} %get-tuple-element.15.forcing, ...), custom_call_target="tpu_custom_call" | custom-call | flops 50000000 | bytes 3866624 | tf_op jit(solution)/shard_map/pallas_call | solution.py:279
  48.6 14.3 %all_to_all.11.sums = f32[8,16,8,128]{3,2,1,0:T(8,128)S(1)} all-to-all(f32[8,16,8,128]{3,2,1,0:T(8,128)S(1)} %get-tuple-element.23), channel_id=1, replica_groups=mesh['z'=8,'place'=8,'space'=4] {'place'}, dimensions={0} | all-to-all | bytes 1048576 | tf_op jit(solution)/shard_map/all_to_all | solution.py:320
  63.0 0.0 copy-start.1
  63.0 4.4 %shard_map.73 = (f32[96,128]{1,0:T(8,128)S(1)}, f32[96,128]{1,0:T(8,128)S(1)}) custom-call(f32[8,16,8,128]{3,2,1,0:T(8,128)S(1)} %all_to_all.11.sums, f32[16,8,128]{2,1,0:T(8,128)S(1)} %get-tuple-element.24.gap, f32[16,8,128]{2,1,0:T(8,128)S(1)} %get-tuple-element.22.carried, f32[13,16,8,128]{3,2,1,0:T(8,128)S(1)} %get-tuple-element.16.fine2, ...), custom_call_target="tpu_custom_call" | custom-call | flops 30000000 | bytes 4096000 | tf_op jit(solution)/shard_map/pallas_call | solution.py:279
  67.4 0.7 collective-permute-start.6
  68.0 3.5 %collective-permute-done.6.got = f32[96,128]{1,0:T(8,128)S(1)} collective-permute-done((f32[96,128]{1,0:T(8,128)S(1)}, f32[96,128]{1,0:T(8,128)S(1)}, u32[]{:S(2)}, u32[]{:S(2)}) %collective-permute-start.6) | collective-permute-done | bytes 49184 | tf_op jit(solution)/shard_map/ppermute | solution.py:328
  71.6 0.0 copy-done.1
  71.6 0.8 %shard_map.74 = (f32[1,2,16,256]{3,2,1,0:T(8,128)}, f32[1,2,16,256]{3,2,1,0:T(8,128)}, f32[1,2,16,256]{3,2,1,0:T(8,128)}) custom-call(f32[96,128]{1,0:T(8,128)S(1)} %collective-permute-done.6.got, f32[96,128]{1,0:T(8,128)S(1)} %get-tuple-element.26.kept, f32[1,2,16,256]{3,2,1,0:T(8,128)S(1)} %copy-done.1), custom_call_target="tpu_custom_call" | custom-call | flops 10000000 | bytes 229376 | tf_op jit(solution)/shard_map/pallas_call | solution.py:279
Async XLA Ops:
  0.6 0.8 %copy-start = (f32[1,2,16,256]{3,2,1,0:T(8,128)S(1)}, f32[1,2,16,256]{3,2,1,0:T(8,128)}, u32[]{:S(2)}) copy-start(f32[1,2,16,256]{3,2,1,0:T(8,128)} %states.3) | copy-start | bytes 98308
  11.5 6.5 %collective-permute-start = (f32[128,128]{1,0:T(8,128)S(1)}, f32[128,128]{1,0:T(8,128)S(1)}, u32[]{:S(2)}, u32[]{:S(2)}) collective-permute-start(f32[128,128]{1,0:T(8,128)S(1)} %bitcast.4), channel_id=1, source_target_pairs={{0,32},{4,36},{8,40},{12,44},{16,48},{20,52},{24,56},{28,60},{32,6... | collective-permute-start | bytes 196616 | tf_op jit(solution)/shard_map/ppermute | solution.py:294
  21.8 15.5 %collective-permute-start.1 = (f32[16,8,128]{2,1,0:T(8,128)S(1)}, f32[16,8,128]{2,1,0:T(8,128)S(1)}, u32[]{:S(2)}, u32[]{:S(2)}) collective-permute-start(f32[16,8,128]{2,1,0:T(8,128)S(1)} %get-tuple-element.20), channel_id=1, source_target_pairs={{0,192},{4,196},{8,200},{12,204},{16,208},{20,212},{24,216},{28,22... | collective-permute-start | bytes 196616 | tf_op jit(solution)/shard_map/ppermute | solution.py:294
  22.5 14.9 %collective-permute-start.2 = (f32[16,8,128]{2,1,0:T(8,128)S(1)}, f32[16,8,128]{2,1,0:T(8,128)S(1)}, u32[]{:S(2)}, u32[]{:S(2)}) collective-permute-start(f32[16,8,128]{2,1,0:T(8,128)S(1)} %get-tuple-element.20), channel_id=1, source_target_pairs={{0,128},{4,132},{8,136},{12,140},{16,144},{20,148},{24,152},{28,15... | collective-permute-start | bytes 196616 | tf_op jit(solution)/shard_map/ppermute | solution.py:294
  30.0 7.7 %collective-permute-start.4 = (f32[128,128]{1,0:T(8,128)S(1)}, f32[128,128]{1,0:T(8,128)S(1)}, u32[]{:S(2)}, u32[]{:S(2)}) collective-permute-start(f32[128,128]{1,0:T(8,128)S(1)} %bitcast.6), channel_id=1, source_target_pairs={{0,4},{4,8},{8,12},{12,16},{16,20},{20,24},{24,28},{28,32},{32,36}... | collective-permute-start | bytes 196616 | tf_op jit(solution)/shard_map/ppermute | solution.py:294
  32.0 8.4 %collective-permute-start.5 = (f32[16,8,128]{2,1,0:T(8,128)S(1)}, f32[16,8,128]{2,1,0:T(8,128)S(1)}, u32[]{:S(2)}, u32[]{:S(2)}) collective-permute-start(f32[16,8,128]{2,1,0:T(8,128)S(1)} %get-tuple-element.22.carried), channel_id=1, source_target_pairs={{0,8},{4,12},{8,16},{12,20},{16,24},{20,28},{24,32},{28,36},{32,40... | collective-permute-start | bytes 196616 | tf_op jit(solution)/shard_map/ppermute | solution.py:294
  35.4 7.5 %collective-permute-start.3 = (f32[16,8,128]{2,1,0:T(8,128)S(1)}, f32[16,8,128]{2,1,0:T(8,128)S(1)}, u32[]{:S(2)}, u32[]{:S(2)}) collective-permute-start(f32[16,8,128]{2,1,0:T(8,128)S(1)} %get-tuple-element.20), channel_id=1, source_target_pairs={{0,64},{4,68},{8,72},{12,76},{16,80},{20,84},{24,88},{28,92},{32,9... | collective-permute-start | bytes 196616 | tf_op jit(solution)/shard_map/ppermute | solution.py:294
  63.0 8.6 %copy-start.1 = (f32[1,2,16,256]{3,2,1,0:T(8,128)S(1)}, f32[1,2,16,256]{3,2,1,0:T(8,128)}, u32[]{:S(2)}) copy-start(f32[1,2,16,256]{3,2,1,0:T(8,128)} %states.3) | copy-start | bytes 98308
  67.4 4.2 %collective-permute-start.6 = (f32[96,128]{1,0:T(8,128)S(1)}, f32[96,128]{1,0:T(8,128)S(1)}, u32[]{:S(2)}, u32[]{:S(2)}) collective-permute-start(f32[96,128]{1,0:T(8,128)S(1)} %get-tuple-element.25), channel_id=1, source_target_pairs={{0,1},{1,0},{2,3},{3,2},{4,5},{5,4},{6,7},{7,6},{8,9},{9,8},{10,11... | collective-permute-start | bytes 147464 | tf_op jit(solution)/shard_map/ppermute | solution.py:328

commit v3 on v2

--- a/solution.py
+++ b/solution.py
@@ -169,8 +169,15 @@
 
 
 def coarse_steps(tiles, count, coarse, planes):
-    turns = jnp.where(lax.axis_index("z") >= planes, count // 3, 0)
-    tiles = lax.fori_loop(0, turns, lambda _, now: apply(now, coarse[2], 3), tiles)
+    turns = jnp.where(lax.axis_index("z") >= planes, count // 9, 0)
+
+    def body(_, now):
+        for _ in range(3):
+            now = apply(now, coarse[2], 3)
+        return now
+
+    tiles = lax.fori_loop(0, turns, body, tiles)
+    count -= count // 9 * 9
     return apply(tiles, coarse[count % 3 - 1], count % 3) if count % 3 else tiles
 
 

time: 72.8 us -> 72.2 us (level)
  no operation moved by 1% of the time
where the time goes in v3:
time: 72.2 us; the launch traced here: 71.8 us
  blocking collectives  24.3 us (34%)
  starting transfers between devices  19.9 us (28%)
  Pallas kernels  16.4 us (23%)
  waiting for transfers between devices  8.85 us (12%)
  other arithmetic  0.92 us (1%)
  local copies, waits for them, and re-layouts  0.76 us (1%)
  between operations  0.76 us (1%)
    ppermute x6, starting transfers between devices, onward(): lax.ppermute(value, axes, [(i, i + steps) for i in range(INTERVALS - step...  19.2 us
    pallas_call x8, Pallas kernels, call(): pl.pallas_call(kernel, out_shape=shapes, in_specs=[VMEM] * len(operands),...  16.4 us
    all_to_all x1, blocking collectives, on_device(): sums = lax.all_to_all(sums, 'place', 0, 0, tiled=True)  14.3 us
    all_to_all x1, blocking collectives, on_device(): whole = lax.all_to_all(pieces, 'space', 0, 0, tiled=True).reshape(128, 128)  9.92 us
    ppermute x6, waiting for transfers between devices, onward(): lax.ppermute(value, axes, [(i, i + steps) for i in range(INTERVALS - step...  5.33 us
    ppermute x1, waiting for transfers between devices, on_device(): lax.ppermute(give, 'space', [(part, part ^ 1) for part in range(PARTS)])  3.53 us
  transfers between devices with their start and end apart: 7, of which 4 were waited for; matrix products, arithmetic and copies ran while one was open for 1% of the time, Pallas kernels for 3%

profile of v3, /device:TPU:64, one launch (start us, length us, event | category | flops | bytes accessed | tf_op | source)
XLA Modules:
  0.0 71.8 jit_solution(15973367058427389487)
XLA Ops:
  0.6 0.0 copy-start
  0.6 0.7 %copy-done = f32[1,2,16,256]{3,2,1,0:T(8,128)S(1)} copy-done((f32[1,2,16,256]{3,2,1,0:T(8,128)S(1)}, f32[1,2,16,256]{3,2,1,0:T(8,128)}, u32[]{:S(2)}) %copy-start) | copy-done | bytes 32792
  1.4 0.2 shard_map.67
  1.6 9.9 %all_to_all.10 = f32[4,32,128]{2,1,0:T(8,128)S(1)} all-to-all(f32[4,32,128]{2,1,0:T(8,128)S(1)} %shard_map.67), channel_id=1, replica_groups=mesh['z'=8,'place'=8,'space'=4] {'space'}, dimensions={0} | all-to-all | bytes 131072 | tf_op jit(solution)/shard_map/all_to_all | solution.py:304
  11.5 3.8 %collective-permute-start = (f32[128,128]{1,0:T(8,128)S(1)}, f32[128,128]{1,0:T(8,128)S(1)}, u32[]{:S(2)}, u32[]{:S(2)}) collective-permute-start(f32[128,128]{1,0:T(8,128)S(1)} %bitcast.4), channel_id=1, source_target_pairs={{0,32},{4,36},{8,40},{12,44},{16,48},{20,52},{24,56},{28,60},{32,6... | collective-permute-start | bytes 196616 | tf_op jit(solution)/shard_map/ppermute | solution.py:301
  15.3 0.9 %pad_add_fusion.tables = s32[3,64,256]{2,1,0:T(8,128)S(1)} fusion(s32[1,64,256]{2,1,0:T(8,128)} %bitcast.8, s32[1,64,256]{2,1,0:T(8,128)} %bitcast.9, s32[1,64,256]{2,1,0:T(8,128)} %bitcast.10), kind=kLoop, calls=%fused_computation | loop fusion | flops 98304 | bytes 393216 | tf_op jit(solution)/shard_map/stack | solution.py:311
  16.2 1.8 %shard_map.68 = (f32[13,16,8,128]{3,2,1,0:T(8,128)S(1)}, f32[5,16,8,128]{3,2,1,0:T(8,128)S(1)}, f32[13,16,8,128]{3,2,1,0:T(8,128)S(1)}, f32[25,16,8,128]{3,2,1,0...) custom-call(f32[128,128]{1,0:T(8,128)S(1)} %bitcast.5, s32[3,64,256]{2,1,0:T(8,128)S(1)} %pad_add_fusion.tables), custom_call_target="tpu_custom_call" | custom-call | flops 10000000 | bytes 4063232 | tf_op jit(solution)/shard_map/pallas_call | solution.py:286
  18.0 0.0 collective-permute-done.behind
  18.0 3.6 %shard_map.69 = (f32[16,8,128]{2,1,0:T(8,128)S(1)}, f32[16,8,128]{2,1,0:T(8,128)S(1)}) custom-call(f32[128,128]{1,0:T(8,128)S(1)} %collective-permute-done.behind, f32[16,8,128]{2,1,0:T(8,128)S(1)} %get-tuple-element.15.forcing, f32[13,16,8,128]{3,2,1,0:T(8,128)S(1)} %get-tuple-element.16.fine2, f32[5,16,8,128]{3,2,1,0:T(8,128)S(1)} %get-tuple-element.17.coarse1, ...), custom_call_target="tpu_custom_call" | custom-call | flops 30000000 | bytes 3932160 | tf_op jit(solution)/shard_map/pallas_call | solution.py:286
  21.6 0.7 collective-permute-start.1
  22.3 7.5 %collective-permute-start.2 = (f32[16,8,128]{2,1,0:T(8,128)S(1)}, f32[16,8,128]{2,1,0:T(8,128)S(1)}, u32[]{:S(2)}, u32[]{:S(2)}) collective-permute-start(f32[16,8,128]{2,1,0:T(8,128)S(1)} %get-tuple-element.20), channel_id=1, source_target_pairs={{0,128},{4,132},{8,136},{12,140},{16,144},{20,148},{24,152},{28,15... | collective-permute-start | bytes 196616 | tf_op jit(solution)/shard_map/ppermute | solution.py:301
  29.8 1.9 %collective-permute-start.4 = (f32[128,128]{1,0:T(8,128)S(1)}, f32[128,128]{1,0:T(8,128)S(1)}, u32[]{:S(2)}, u32[]{:S(2)}) collective-permute-start(f32[128,128]{1,0:T(8,128)S(1)} %bitcast.6), channel_id=1, source_target_pairs={{0,4},{4,8},{8,12},{12,16},{16,20},{20,24},{24,28},{28,32},{32,36}... | collective-permute-start | bytes 196616 | tf_op jit(solution)/shard_map/ppermute | solution.py:301
  31.8 3.4 %collective-permute-start.5 = (f32[16,8,128]{2,1,0:T(8,128)S(1)}, f32[16,8,128]{2,1,0:T(8,128)S(1)}, u32[]{:S(2)}, u32[]{:S(2)}) collective-permute-start(f32[16,8,128]{2,1,0:T(8,128)S(1)} %get-tuple-element.22.carried), channel_id=1, source_target_pairs={{0,8},{4,12},{8,16},{12,20},{16,24},{20,28},{24,32},{28,36},{32,40... | collective-permute-start | bytes 196616 | tf_op jit(solution)/shard_map/ppermute | solution.py:301
  35.2 1.9 %collective-permute-start.3 = (f32[16,8,128]{2,1,0:T(8,128)S(1)}, f32[16,8,128]{2,1,0:T(8,128)S(1)}, u32[]{:S(2)}, u32[]{:S(2)}) collective-permute-start(f32[16,8,128]{2,1,0:T(8,128)S(1)} %get-tuple-element.20), channel_id=1, source_target_pairs={{0,64},{4,68},{8,72},{12,76},{16,80},{20,84},{24,88},{28,92},{32,9... | collective-permute-start | bytes 196616 | tf_op jit(solution)/shard_map/ppermute | solution.py:301
  37.1 0.0 collective-permute-done.1.sixth
  37.1 0.1 shard_map.70.far
  37.2 0.0 collective-permute-done.2.fourth
  37.2 0.1 shard_map.71.near
  37.4 0.2 collective-permute-done.4.last
  37.5 2.6 %collective-permute-done.5.ahead = f32[16,8,128]{2,1,0:T(8,128)S(1)} collective-permute-done((f32[16,8,128]{2,1,0:T(8,128)S(1)}, f32[16,8,128]{2,1,0:T(8,128)S(1)}, u32[]{:S(2)}, u32[]{:S(2)}) %collective-permute-start.5) | collective-permute-done | bytes 65568 | tf_op jit(solution)/shard_map/ppermute | solution.py:301
  40.2 2.5 %collective-permute-done.3.second = f32[16,8,128]{2,1,0:T(8,128)S(1)} collective-permute-done((f32[16,8,128]{2,1,0:T(8,128)S(1)}, f32[16,8,128]{2,1,0:T(8,128)S(1)}, u32[]{:S(2)}, u32[]{:S(2)}) %collective-permute-start.3) | collective-permute-done | bytes 65568 | tf_op jit(solution)/shard_map/ppermute | solution.py:301
  42.7 5.4 %shard_map.72 = (f32[8,16,8,128]{3,2,1,0:T(8,128)S(1)}, f32[16,8,128]{2,1,0:T(8,128)S(1)}) custom-call(f32[16,8,128]{2,1,0:T(8,128)S(1)} %shard_map.71.near, f32[16,8,128]{2,1,0:T(8,128)S(1)} %collective-permute-done.3.second, f32[16,8,128]{2,1,0:T(8,128)S(1)} %get-tuple-element.21.before, f32[16,8,128]{2,1,0:T(8,128)S(1)} %get-tuple-element.15.forcing, ...), custom_call_target="tpu_custom_call" | custom-call | flops 50000000 | bytes 3866624 | tf_op jit(solution)/shard_map/pallas_call | solution.py:286
  48.1 14.3 %all_to_all.11.sums = f32[8,16,8,128]{3,2,1,0:T(8,128)S(1)} all-to-all(f32[8,16,8,128]{3,2,1,0:T(8,128)S(1)} %get-tuple-element.23), channel_id=1, replica_groups=mesh['z'=8,'place'=8,'space'=4] {'place'}, dimensions={0} | all-to-all | bytes 1048576 | tf_op jit(solution)/shard_map/all_to_all | solution.py:327
  62.4 0.0 copy-start.1
  62.4 4.4 %shard_map.73 = (f32[96,128]{1,0:T(8,128)S(1)}, f32[96,128]{1,0:T(8,128)S(1)}) custom-call(f32[8,16,8,128]{3,2,1,0:T(8,128)S(1)} %all_to_all.11.sums, f32[16,8,128]{2,1,0:T(8,128)S(1)} %get-tuple-element.24.gap, f32[16,8,128]{2,1,0:T(8,128)S(1)} %get-tuple-element.22.carried, f32[13,16,8,128]{3,2,1,0:T(8,128)S(1)} %get-tuple-element.16.fine2, ...), custom_call_target="tpu_custom_call" | custom-call | flops 30000000 | bytes 4096000 | tf_op jit(solution)/shard_map/pallas_call | solution.py:286
  66.8 0.7 collective-permute-start.6
  67.5 3.5 %collective-permute-done.6.got = f32[96,128]{1,0:T(8,128)S(1)} collective-permute-done((f32[96,128]{1,0:T(8,128)S(1)}, f32[96,128]{1,0:T(8,128)S(1)}, u32[]{:S(2)}, u32[]{:S(2)}) %collective-permute-start.6) | collective-permute-done | bytes 49184 | tf_op jit(solution)/shard_map/ppermute | solution.py:335
  71.0 0.0 copy-done.1
  71.0 0.8 %shard_map.74 = (f32[1,2,16,256]{3,2,1,0:T(8,128)}, f32[1,2,16,256]{3,2,1,0:T(8,128)}, f32[1,2,16,256]{3,2,1,0:T(8,128)}) custom-call(f32[96,128]{1,0:T(8,128)S(1)} %collective-permute-done.6.got, f32[96,128]{1,0:T(8,128)S(1)} %get-tuple-element.26.kept, f32[1,2,16,256]{3,2,1,0:T(8,128)S(1)} %copy-done.1), custom_call_target="tpu_custom_call" | custom-call | flops 10000000 | bytes 229376 | tf_op jit(solution)/shard_map/pallas_call | solution.py:286
Async XLA Ops:
  0.6 0.8 %copy-start = (f32[1,2,16,256]{3,2,1,0:T(8,128)S(1)}, f32[1,2,16,256]{3,2,1,0:T(8,128)}, u32[]{:S(2)}) copy-start(f32[1,2,16,256]{3,2,1,0:T(8,128)} %states.3) | copy-start | bytes 98308
  11.5 6.5 %collective-permute-start = (f32[128,128]{1,0:T(8,128)S(1)}, f32[128,128]{1,0:T(8,128)S(1)}, u32[]{:S(2)}, u32[]{:S(2)}) collective-permute-start(f32[128,128]{1,0:T(8,128)S(1)} %bitcast.4), channel_id=1, source_target_pairs={{0,32},{4,36},{8,40},{12,44},{16,48},{20,52},{24,56},{28,60},{32,6... | collective-permute-start | bytes 196616 | tf_op jit(solution)/shard_map/ppermute | solution.py:301
  21.6 15.5 %collective-permute-start.1 = (f32[16,8,128]{2,1,0:T(8,128)S(1)}, f32[16,8,128]{2,1,0:T(8,128)S(1)}, u32[]{:S(2)}, u32[]{:S(2)}) collective-permute-start(f32[16,8,128]{2,1,0:T(8,128)S(1)} %get-tuple-element.20), channel_id=1, source_target_pairs={{0,192},{4,196},{8,200},{12,204},{16,208},{20,212},{24,216},{28,22... | collective-permute-start | bytes 196616 | tf_op jit(solution)/shard_map/ppermute | solution.py:301
  22.3 14.9 %collective-permute-start.2 = (f32[16,8,128]{2,1,0:T(8,128)S(1)}, f32[16,8,128]{2,1,0:T(8,128)S(1)}, u32[]{:S(2)}, u32[]{:S(2)}) collective-permute-start(f32[16,8,128]{2,1,0:T(8,128)S(1)} %get-tuple-element.20), channel_id=1, source_target_pairs={{0,128},{4,132},{8,136},{12,140},{16,144},{20,148},{24,152},{28,15... | collective-permute-start | bytes 196616 | tf_op jit(solution)/shard_map/ppermute | solution.py:301
  29.8 7.7 %collective-permute-start.4 = (f32[128,128]{1,0:T(8,128)S(1)}, f32[128,128]{1,0:T(8,128)S(1)}, u32[]{:S(2)}, u32[]{:S(2)}) collective-permute-start(f32[128,128]{1,0:T(8,128)S(1)} %bitcast.6), channel_id=1, source_target_pairs={{0,4},{4,8},{8,12},{12,16},{16,20},{20,24},{24,28},{28,32},{32,36}... | collective-permute-start | bytes 196616 | tf_op jit(solution)/shard_map/ppermute | solution.py:301
  31.8 8.4 %collective-permute-start.5 = (f32[16,8,128]{2,1,0:T(8,128)S(1)}, f32[16,8,128]{2,1,0:T(8,128)S(1)}, u32[]{:S(2)}, u32[]{:S(2)}) collective-permute-start(f32[16,8,128]{2,1,0:T(8,128)S(1)} %get-tuple-element.22.carried), channel_id=1, source_target_pairs={{0,8},{4,12},{8,16},{12,20},{16,24},{20,28},{24,32},{28,36},{32,40... | collective-permute-start | bytes 196616 | tf_op jit(solution)/shard_map/ppermute | solution.py:301
  35.2 7.5 %collective-permute-start.3 = (f32[16,8,128]{2,1,0:T(8,128)S(1)}, f32[16,8,128]{2,1,0:T(8,128)S(1)}, u32[]{:S(2)}, u32[]{:S(2)}) collective-permute-start(f32[16,8,128]{2,1,0:T(8,128)S(1)} %get-tuple-element.20), channel_id=1, source_target_pairs={{0,64},{4,68},{8,72},{12,76},{16,80},{20,84},{24,88},{28,92},{32,9... | collective-permute-start | bytes 196616 | tf_op jit(solution)/shard_map/ppermute | solution.py:301
  62.4 8.6 %copy-start.1 = (f32[1,2,16,256]{3,2,1,0:T(8,128)S(1)}, f32[1,2,16,256]{3,2,1,0:T(8,128)}, u32[]{:S(2)}) copy-start(f32[1,2,16,256]{3,2,1,0:T(8,128)} %states.3) | copy-start | bytes 98308
  66.8 4.2 %collective-permute-start.6 = (f32[96,128]{1,0:T(8,128)S(1)}, f32[96,128]{1,0:T(8,128)S(1)}, u32[]{:S(2)}, u32[]{:S(2)}) collective-permute-start(f32[96,128]{1,0:T(8,128)S(1)} %get-tuple-element.25), channel_id=1, source_target_pairs={{0,1},{1,0},{2,3},{3,2},{4,5},{5,4},{6,7},{7,6},{8,9},{9,8},{10,11... | collective-permute-start | bytes 147464 | tf_op jit(solution)/shard_map/ppermute | solution.py:335

commit v4 on v3

--- a/solution.py
+++ b/solution.py
@@ -168,8 +168,9 @@
     return lax.fori_loop(0, STEPS // 2, lambda _, now: tuple(apply(field, fine2, 2) for field in now), fields)
 
 
-def coarse_steps(tiles, count, coarse, planes):
-    turns = jnp.where(lax.axis_index("z") >= planes, count // 9, 0)
+def coarse_steps(tiles, count, coarse, planes, end=PLANES):
+    plane = lax.axis_index("z")
+    turns = jnp.where((plane >= planes) & (plane < end), count // 9, 0)
 
     def body(_, now):
         for _ in range(3):
@@ -211,7 +212,7 @@
     coarse = (coarse1, coarse2, coarse3)
     _, forced = force(load_flat(behind), where_me() == PLACES, fine2, coarse)
     store_tiles(before, forced)
-    store_tiles(pair, added(coarse_steps(forced, 64, coarse, 1), load_tiles(forcing)))
+    store_tiles(pair, added(coarse_steps(forced, 64, coarse, 1, PLANES - 2), load_tiles(forcing)))
 
 
 def far_kernel(sixth, coarse1, coarse2, coarse3, out):

time: 72.2 us -> 70.4 us (0.975)
  starting transfers between devices: 19.9 us -> 18.9 us
  waiting for transfers between devices: 8.85 us -> 7.97 us
    ppermute x6, starting transfers between devices: 19.2 us -> 18.3 us  [onward(): lax.ppermute(value, axes, [(i, i + steps) for i in range(INTERVALS - step...]
    ppermute x6, waiting for transfers between devices: 5.33 us -> 4.45 us  [onward(): lax.ppermute(value, axes, [(i, i + steps) for i in range(INTERVALS - step...]
  transfers between devices with their start and end apart: 7 -> 7, of which waited for: 4 -> 3; matrix products, arithmetic and copies ran while one was open for 1% -> 1% of each run, Pallas kernels for 3% -> 3%
where the time goes in v4:
time: 70.4 us; the launch traced here: 70 us
  blocking collectives  24.2 us (34%)
  starting transfers between devices  18.9 us (27%)
  Pallas kernels  16.4 us (23%)
  waiting for transfers between devices  7.97 us (11%)
  other arithmetic  0.92 us (1%)
  between operations  0.77 us (1%)
  local copies, waits for them, and re-layouts  0.76 us (1%)
    ppermute x6, starting transfers between devices, onward(): lax.ppermute(value, axes, [(i, i + steps) for i in range(INTERVALS - step...  18.3 us
    pallas_call x8, Pallas kernels, call(): pl.pallas_call(kernel, out_shape=shapes, in_specs=[VMEM] * len(operands),...  16.4 us
    all_to_all x1, blocking collectives, on_device(): sums = lax.all_to_all(sums, 'place', 0, 0, tiled=True)  14.3 us
    all_to_all x1, blocking collectives, on_device(): whole = lax.all_to_all(pieces, 'space', 0, 0, tiled=True).reshape(128, 128)  9.92 us
    ppermute x6, waiting for transfers between devices, onward(): lax.ppermute(value, axes, [(i, i + steps) for i in range(INTERVALS - step...  4.45 us
    ppermute x1, waiting for transfers between devices, on_device(): lax.ppermute(give, 'space', [(part, part ^ 1) for part in range(PARTS)])  3.53 us
  transfers between devices with their start and end apart: 7, of which 3 were waited for; matrix products, arithmetic and copies ran while one was open for 1% of the time, Pallas kernels for 3%

profile of v4, /device:TPU:64, one launch (start us, length us, event | category | flops | bytes accessed | tf_op | source)
XLA Modules:
  0.0 70.0 jit_solution(15988169193231587638)
XLA Ops:
  0.6 0.0 copy-start
  0.6 0.7 %copy-done = f32[1,2,16,256]{3,2,1,0:T(8,128)S(1)} copy-done((f32[1,2,16,256]{3,2,1,0:T(8,128)S(1)}, f32[1,2,16,256]{3,2,1,0:T(8,128)}, u32[]{:S(2)}) %copy-start) | copy-done | bytes 32792
  1.4 0.2 shard_map.67
  1.6 9.9 %all_to_all.10 = f32[4,32,128]{2,1,0:T(8,128)S(1)} all-to-all(f32[4,32,128]{2,1,0:T(8,128)S(1)} %shard_map.67), channel_id=1, replica_groups=mesh['z'=8,'place'=8,'space'=4] {'space'}, dimensions={0} | all-to-all | bytes 131072 | tf_op jit(solution)/shard_map/all_to_all | solution.py:305
  11.5 3.8 %collective-permute-start = (f32[128,128]{1,0:T(8,128)S(1)}, f32[128,128]{1,0:T(8,128)S(1)}, u32[]{:S(2)}, u32[]{:S(2)}) collective-permute-start(f32[128,128]{1,0:T(8,128)S(1)} %bitcast.4), channel_id=1, source_target_pairs={{0,32},{4,36},{8,40},{12,44},{16,48},{20,52},{24,56},{28,60},{32,6... | collective-permute-start | bytes 196616 | tf_op jit(solution)/shard_map/ppermute | solution.py:302
  15.3 0.9 %pad_add_fusion.tables = s32[3,64,256]{2,1,0:T(8,128)S(1)} fusion(s32[1,64,256]{2,1,0:T(8,128)} %bitcast.8, s32[1,64,256]{2,1,0:T(8,128)} %bitcast.9, s32[1,64,256]{2,1,0:T(8,128)} %bitcast.10), kind=kLoop, calls=%fused_computation | loop fusion | flops 98304 | bytes 393216 | tf_op jit(solution)/shard_map/stack | solution.py:312
  16.2 1.8 %shard_map.68 = (f32[13,16,8,128]{3,2,1,0:T(8,128)S(1)}, f32[5,16,8,128]{3,2,1,0:T(8,128)S(1)}, f32[13,16,8,128]{3,2,1,0:T(8,128)S(1)}, f32[25,16,8,128]{3,2,1,0...) custom-call(f32[128,128]{1,0:T(8,128)S(1)} %bitcast.5, s32[3,64,256]{2,1,0:T(8,128)S(1)} %pad_add_fusion.tables), custom_call_target="tpu_custom_call" | custom-call | flops 10000000 | bytes 4063232 | tf_op jit(solution)/shard_map/pallas_call | solution.py:287
  18.0 0.0 collective-permute-done.behind
  18.0 3.6 %shard_map.69 = (f32[16,8,128]{2,1,0:T(8,128)S(1)}, f32[16,8,128]{2,1,0:T(8,128)S(1)}) custom-call(f32[128,128]{1,0:T(8,128)S(1)} %collective-permute-done.behind, f32[16,8,128]{2,1,0:T(8,128)S(1)} %get-tuple-element.15.forcing, f32[13,16,8,128]{3,2,1,0:T(8,128)S(1)} %get-tuple-element.16.fine2, f32[5,16,8,128]{3,2,1,0:T(8,128)S(1)} %get-tuple-element.17.coarse1, ...), custom_call_target="tpu_custom_call" | custom-call | flops 30000000 | bytes 3932160 | tf_op jit(solution)/shard_map/pallas_call | solution.py:287
  21.6 0.7 collective-permute-start.1
  22.3 4.9 %collective-permute-start.2 = (f32[16,8,128]{2,1,0:T(8,128)S(1)}, f32[16,8,128]{2,1,0:T(8,128)S(1)}, u32[]{:S(2)}, u32[]{:S(2)}) collective-permute-start(f32[16,8,128]{2,1,0:T(8,128)S(1)} %get-tuple-element.20), channel_id=1, source_target_pairs={{0,128},{4,132},{8,136},{12,140},{16,144},{20,148},{24,152},{28,15... | collective-permute-start | bytes 196616 | tf_op jit(solution)/shard_map/ppermute | solution.py:302
  27.2 1.9 %collective-permute-start.4 = (f32[128,128]{1,0:T(8,128)S(1)}, f32[128,128]{1,0:T(8,128)S(1)}, u32[]{:S(2)}, u32[]{:S(2)}) collective-permute-start(f32[128,128]{1,0:T(8,128)S(1)} %bitcast.6), channel_id=1, source_target_pairs={{0,4},{4,8},{8,12},{12,16},{16,20},{20,24},{24,28},{28,32},{32,36}... | collective-permute-start | bytes 196616 | tf_op jit(solution)/shard_map/ppermute | solution.py:302
  29.2 3.4 %collective-permute-start.5 = (f32[16,8,128]{2,1,0:T(8,128)S(1)}, f32[16,8,128]{2,1,0:T(8,128)S(1)}, u32[]{:S(2)}, u32[]{:S(2)}) collective-permute-start(f32[16,8,128]{2,1,0:T(8,128)S(1)} %get-tuple-element.22.carried), channel_id=1, source_target_pairs={{0,8},{4,12},{8,16},{12,20},{16,24},{20,28},{24,32},{28,36},{32,40... | collective-permute-start | bytes 196616 | tf_op jit(solution)/shard_map/ppermute | solution.py:302
  32.6 3.6 %collective-permute-start.3 = (f32[16,8,128]{2,1,0:T(8,128)S(1)}, f32[16,8,128]{2,1,0:T(8,128)S(1)}, u32[]{:S(2)}, u32[]{:S(2)}) collective-permute-start(f32[16,8,128]{2,1,0:T(8,128)S(1)} %get-tuple-element.20), channel_id=1, source_target_pairs={{0,64},{4,68},{8,72},{12,76},{16,80},{20,84},{24,88},{28,92},{32,9... | collective-permute-start | bytes 196616 | tf_op jit(solution)/shard_map/ppermute | solution.py:302
  36.1 0.0 collective-permute-done.1.sixth
  36.2 0.1 shard_map.70.far
  36.3 0.0 collective-permute-done.2.fourth
  36.3 0.1 shard_map.71.near
  36.4 0.0 collective-permute-done.4.last
  36.4 2.4 %collective-permute-done.5.ahead = f32[16,8,128]{2,1,0:T(8,128)S(1)} collective-permute-done((f32[16,8,128]{2,1,0:T(8,128)S(1)}, f32[16,8,128]{2,1,0:T(8,128)S(1)}, u32[]{:S(2)}, u32[]{:S(2)}) %collective-permute-start.5) | collective-permute-done | bytes 65568 | tf_op jit(solution)/shard_map/ppermute | solution.py:302
  38.8 2.1 %collective-permute-done.3.second = f32[16,8,128]{2,1,0:T(8,128)S(1)} collective-permute-done((f32[16,8,128]{2,1,0:T(8,128)S(1)}, f32[16,8,128]{2,1,0:T(8,128)S(1)}, u32[]{:S(2)}, u32[]{:S(2)}) %collective-permute-start.3) | collective-permute-done | bytes 65568 | tf_op jit(solution)/shard_map/ppermute | solution.py:302
  40.9 5.4 %shard_map.72 = (f32[8,16,8,128]{3,2,1,0:T(8,128)S(1)}, f32[16,8,128]{2,1,0:T(8,128)S(1)}) custom-call(f32[16,8,128]{2,1,0:T(8,128)S(1)} %shard_map.71.near, f32[16,8,128]{2,1,0:T(8,128)S(1)} %collective-permute-done.3.second, f32[16,8,128]{2,1,0:T(8,128)S(1)} %get-tuple-element.21.before, f32[16,8,128]{2,1,0:T(8,128)S(1)} %get-tuple-element.15.forcing, ...), custom_call_target="tpu_custom_call" | custom-call | flops 50000000 | bytes 3866624 | tf_op jit(solution)/shard_map/pallas_call | solution.py:287
  46.2 14.3 %all_to_all.11.sums = f32[8,16,8,128]{3,2,1,0:T(8,128)S(1)} all-to-all(f32[8,16,8,128]{3,2,1,0:T(8,128)S(1)} %get-tuple-element.23), channel_id=1, replica_groups=mesh['z'=8,'place'=8,'space'=4] {'place'}, dimensions={0} | all-to-all | bytes 1048576 | tf_op jit(solution)/shard_map/all_to_all | solution.py:328
  60.5 0.0 copy-start.1
  60.5 4.4 %shard_map.73 = (f32[96,128]{1,0:T(8,128)S(1)}, f32[96,128]{1,0:T(8,128)S(1)}) custom-call(f32[8,16,8,128]{3,2,1,0:T(8,128)S(1)} %all_to_all.11.sums, f32[16,8,128]{2,1,0:T(8,128)S(1)} %get-tuple-element.24.gap, f32[16,8,128]{2,1,0:T(8,128)S(1)} %get-tuple-element.22.carried, f32[13,16,8,128]{3,2,1,0:T(8,128)S(1)} %get-tuple-element.16.fine2, ...), custom_call_target="tpu_custom_call" | custom-call | flops 30000000 | bytes 4096000 | tf_op jit(solution)/shard_map/pallas_call | solution.py:287
  64.9 0.7 collective-permute-start.6
  65.6 3.5 %collective-permute-done.6.got = f32[96,128]{1,0:T(8,128)S(1)} collective-permute-done((f32[96,128]{1,0:T(8,128)S(1)}, f32[96,128]{1,0:T(8,128)S(1)}, u32[]{:S(2)}, u32[]{:S(2)}) %collective-permute-start.6) | collective-permute-done | bytes 49184 | tf_op jit(solution)/shard_map/ppermute | solution.py:336
  69.1 0.0 copy-done.1
  69.1 0.8 %shard_map.74 = (f32[1,2,16,256]{3,2,1,0:T(8,128)}, f32[1,2,16,256]{3,2,1,0:T(8,128)}, f32[1,2,16,256]{3,2,1,0:T(8,128)}) custom-call(f32[96,128]{1,0:T(8,128)S(1)} %collective-permute-done.6.got, f32[96,128]{1,0:T(8,128)S(1)} %get-tuple-element.26.kept, f32[1,2,16,256]{3,2,1,0:T(8,128)S(1)} %copy-done.1), custom_call_target="tpu_custom_call" | custom-call | flops 10000000 | bytes 229376 | tf_op jit(solution)/shard_map/pallas_call | solution.py:287
Async XLA Ops:
  0.6 0.8 %copy-start = (f32[1,2,16,256]{3,2,1,0:T(8,128)S(1)}, f32[1,2,16,256]{3,2,1,0:T(8,128)}, u32[]{:S(2)}) copy-start(f32[1,2,16,256]{3,2,1,0:T(8,128)} %states.3) | copy-start | bytes 98308
  11.5 6.5 %collective-permute-start = (f32[128,128]{1,0:T(8,128)S(1)}, f32[128,128]{1,0:T(8,128)S(1)}, u32[]{:S(2)}, u32[]{:S(2)}) collective-permute-start(f32[128,128]{1,0:T(8,128)S(1)} %bitcast.4), channel_id=1, source_target_pairs={{0,32},{4,36},{8,40},{12,44},{16,48},{20,52},{24,56},{28,60},{32,6... | collective-permute-start | bytes 196616 | tf_op jit(solution)/shard_map/ppermute | solution.py:302
  21.6 14.5 %collective-permute-start.1 = (f32[16,8,128]{2,1,0:T(8,128)S(1)}, f32[16,8,128]{2,1,0:T(8,128)S(1)}, u32[]{:S(2)}, u32[]{:S(2)}) collective-permute-start(f32[16,8,128]{2,1,0:T(8,128)S(1)} %get-tuple-element.20), channel_id=1, source_target_pairs={{0,192},{4,196},{8,200},{12,204},{16,208},{20,212},{24,216},{28,22... | collective-permute-start | bytes 196616 | tf_op jit(solution)/shard_map/ppermute | solution.py:302
  22.3 14.0 %collective-permute-start.2 = (f32[16,8,128]{2,1,0:T(8,128)S(1)}, f32[16,8,128]{2,1,0:T(8,128)S(1)}, u32[]{:S(2)}, u32[]{:S(2)}) collective-permute-start(f32[16,8,128]{2,1,0:T(8,128)S(1)} %get-tuple-element.20), channel_id=1, source_target_pairs={{0,128},{4,132},{8,136},{12,140},{16,144},{20,148},{24,152},{28,15... | collective-permute-start | bytes 196616 | tf_op jit(solution)/shard_map/ppermute | solution.py:302
  27.2 9.2 %collective-permute-start.4 = (f32[128,128]{1,0:T(8,128)S(1)}, f32[128,128]{1,0:T(8,128)S(1)}, u32[]{:S(2)}, u32[]{:S(2)}) collective-permute-start(f32[128,128]{1,0:T(8,128)S(1)} %bitcast.6), channel_id=1, source_target_pairs={{0,4},{4,8},{8,12},{12,16},{16,20},{20,24},{24,28},{28,32},{32,36}... | collective-permute-start | bytes 196616 | tf_op jit(solution)/shard_map/ppermute | solution.py:302
  29.2 9.6 %collective-permute-start.5 = (f32[16,8,128]{2,1,0:T(8,128)S(1)}, f32[16,8,128]{2,1,0:T(8,128)S(1)}, u32[]{:S(2)}, u32[]{:S(2)}) collective-permute-start(f32[16,8,128]{2,1,0:T(8,128)S(1)} %get-tuple-element.22.carried), channel_id=1, source_target_pairs={{0,8},{4,12},{8,16},{12,20},{16,24},{20,28},{24,32},{28,36},{32,40... | collective-permute-start | bytes 196616 | tf_op jit(solution)/shard_map/ppermute | solution.py:302
  32.6 8.3 %collective-permute-start.3 = (f32[16,8,128]{2,1,0:T(8,128)S(1)}, f32[16,8,128]{2,1,0:T(8,128)S(1)}, u32[]{:S(2)}, u32[]{:S(2)}) collective-permute-start(f32[16,8,128]{2,1,0:T(8,128)S(1)} %get-tuple-element.20), channel_id=1, source_target_pairs={{0,64},{4,68},{8,72},{12,76},{16,80},{20,84},{24,88},{28,92},{32,9... | collective-permute-start | bytes 196616 | tf_op jit(solution)/shard_map/ppermute | solution.py:302
  60.5 8.6 %copy-start.1 = (f32[1,2,16,256]{3,2,1,0:T(8,128)S(1)}, f32[1,2,16,256]{3,2,1,0:T(8,128)}, u32[]{:S(2)}) copy-start(f32[1,2,16,256]{3,2,1,0:T(8,128)} %states.3) | copy-start | bytes 98308
  64.9 4.2 %collective-permute-start.6 = (f32[96,128]{1,0:T(8,128)S(1)}, f32[96,128]{1,0:T(8,128)S(1)}, u32[]{:S(2)}, u32[]{:S(2)}) collective-permute-start(f32[96,128]{1,0:T(8,128)S(1)} %get-tuple-element.25), channel_id=1, source_target_pairs={{0,1},{1,0},{2,3},{3,2},{4,5},{5,4},{6,7},{7,6},{8,9},{9,8},{10,11... | collective-permute-start | bytes 147464 | tf_op jit(solution)/shard_map/ppermute | solution.py:336

commit v5 on v4

--- a/solution.py
+++ b/solution.py
@@ -170,15 +170,15 @@
 
 def coarse_steps(tiles, count, coarse, planes, end=PLANES):
     plane = lax.axis_index("z")
-    turns = jnp.where((plane >= planes) & (plane < end), count // 9, 0)
+    turns = jnp.where((plane >= planes) & (plane < end), count // 21, 0)
 
     def body(_, now):
-        for _ in range(3):
+        for _ in range(7):
             now = apply(now, coarse[2], 3)
         return now
 
     tiles = lax.fori_loop(0, turns, body, tiles)
-    count -= count // 9 * 9
+    count -= count // 21 * 21
     return apply(tiles, coarse[count % 3 - 1], count % 3) if count % 3 else tiles
 
 

time: 70.4 us -> 70.6 us (level)
  no operation moved by 1% of the time
where the time goes in v5:
time: 70.6 us; the launch traced here: 70.2 us
  blocking collectives  24.2 us (34%)
  starting transfers between devices  18.9 us (27%)
  Pallas kernels  16.6 us (24%)
  waiting for transfers between devices  7.97 us (11%)
  other arithmetic  0.92 us (1%)
  between operations  0.77 us (1%)
  local copies, waits for them, and re-layouts  0.76 us (1%)
    ppermute x6, starting transfers between devices, onward(): lax.ppermute(value, axes, [(i, i + steps) for i in range(INTERVALS - step...  18.3 us
    pallas_call x8, Pallas kernels, call(): pl.pallas_call(kernel, out_shape=shapes, in_specs=[VMEM] * len(operands),...  16.6 us
    all_to_all x1, blocking collectives, on_device(): sums = lax.all_to_all(sums, 'place', 0, 0, tiled=True)  14.3 us
    all_to_all x1, blocking collectives, on_device(): whole = lax.all_to_all(pieces, 'space', 0, 0, tiled=True).reshape(128, 128)  9.92 us
    ppermute x6, waiting for transfers between devices, onward(): lax.ppermute(value, axes, [(i, i + steps) for i in range(INTERVALS - step...  4.45 us
    ppermute x1, waiting for transfers between devices, on_device(): lax.ppermute(give, 'space', [(part, part ^ 1) for part in range(PARTS)])  3.53 us
  transfers between devices with their start and end apart: 7, of which 3 were waited for; matrix products, arithmetic and copies ran while one was open for 1% of the time, Pallas kernels for 3%

profile of v5, /device:TPU:64, one launch (start us, length us, event | category | flops | bytes accessed | tf_op | source)
XLA Modules:
  0.0 70.2 jit_solution(16802807606540263898)
XLA Ops:
  0.6 0.0 copy-start
  0.6 0.7 %copy-done = f32[1,2,16,256]{3,2,1,0:T(8,128)S(1)} copy-done((f32[1,2,16,256]{3,2,1,0:T(8,128)S(1)}, f32[1,2,16,256]{3,2,1,0:T(8,128)}, u32[]{:S(2)}) %copy-start) | copy-done | bytes 32792
  1.4 0.2 shard_map.67
  1.6 9.9 %all_to_all.10 = f32[4,32,128]{2,1,0:T(8,128)S(1)} all-to-all(f32[4,32,128]{2,1,0:T(8,128)S(1)} %shard_map.67), channel_id=1, replica_groups=mesh['z'=8,'place'=8,'space'=4] {'space'}, dimensions={0} | all-to-all | bytes 131072 | tf_op jit(solution)/shard_map/all_to_all | solution.py:305
  11.5 3.8 %collective-permute-start = (f32[128,128]{1,0:T(8,128)S(1)}, f32[128,128]{1,0:T(8,128)S(1)}, u32[]{:S(2)}, u32[]{:S(2)}) collective-permute-start(f32[128,128]{1,0:T(8,128)S(1)} %bitcast.4), channel_id=1, source_target_pairs={{0,32},{4,36},{8,40},{12,44},{16,48},{20,52},{24,56},{28,60},{32,6... | collective-permute-start | bytes 196616 | tf_op jit(solution)/shard_map/ppermute | solution.py:302
  15.3 0.9 %pad_add_fusion.tables = s32[3,64,256]{2,1,0:T(8,128)S(1)} fusion(s32[1,64,256]{2,1,0:T(8,128)} %bitcast.8, s32[1,64,256]{2,1,0:T(8,128)} %bitcast.9, s32[1,64,256]{2,1,0:T(8,128)} %bitcast.10), kind=kLoop, calls=%fused_computation | loop fusion | flops 98304 | bytes 393216 | tf_op jit(solution)/shard_map/stack | solution.py:312
  16.2 1.8 %shard_map.68 = (f32[13,16,8,128]{3,2,1,0:T(8,128)S(1)}, f32[5,16,8,128]{3,2,1,0:T(8,128)S(1)}, f32[13,16,8,128]{3,2,1,0:T(8,128)S(1)}, f32[25,16,8,128]{3,2,1,0...) custom-call(f32[128,128]{1,0:T(8,128)S(1)} %bitcast.5, s32[3,64,256]{2,1,0:T(8,128)S(1)} %pad_add_fusion.tables), custom_call_target="tpu_custom_call" | custom-call | flops 10000000 | bytes 4063232 | tf_op jit(solution)/shard_map/pallas_call | solution.py:287
  18.0 0.0 collective-permute-done.behind
  18.0 3.7 %shard_map.69 = (f32[16,8,128]{2,1,0:T(8,128)S(1)}, f32[16,8,128]{2,1,0:T(8,128)S(1)}) custom-call(f32[128,128]{1,0:T(8,128)S(1)} %collective-permute-done.behind, f32[16,8,128]{2,1,0:T(8,128)S(1)} %get-tuple-element.15.forcing, f32[13,16,8,128]{3,2,1,0:T(8,128)S(1)} %get-tuple-element.16.fine2, f32[5,16,8,128]{3,2,1,0:T(8,128)S(1)} %get-tuple-element.17.coarse1, ...), custom_call_target="tpu_custom_call" | custom-call | flops 30000000 | bytes 3932160 | tf_op jit(solution)/shard_map/pallas_call | solution.py:287
  21.7 0.7 collective-permute-start.1
  22.4 4.9 %collective-permute-start.2 = (f32[16,8,128]{2,1,0:T(8,128)S(1)}, f32[16,8,128]{2,1,0:T(8,128)S(1)}, u32[]{:S(2)}, u32[]{:S(2)}) collective-permute-start(f32[16,8,128]{2,1,0:T(8,128)S(1)} %get-tuple-element.20), channel_id=1, source_target_pairs={{0,128},{4,132},{8,136},{12,140},{16,144},{20,148},{24,152},{28,15... | collective-permute-start | bytes 196616 | tf_op jit(solution)/shard_map/ppermute | solution.py:302
  27.2 1.9 %collective-permute-start.4 = (f32[128,128]{1,0:T(8,128)S(1)}, f32[128,128]{1,0:T(8,128)S(1)}, u32[]{:S(2)}, u32[]{:S(2)}) collective-permute-start(f32[128,128]{1,0:T(8,128)S(1)} %bitcast.6), channel_id=1, source_target_pairs={{0,4},{4,8},{8,12},{12,16},{16,20},{20,24},{24,28},{28,32},{32,36}... | collective-permute-start | bytes 196616 | tf_op jit(solution)/shard_map/ppermute | solution.py:302
  29.2 3.4 %collective-permute-start.5 = (f32[16,8,128]{2,1,0:T(8,128)S(1)}, f32[16,8,128]{2,1,0:T(8,128)S(1)}, u32[]{:S(2)}, u32[]{:S(2)}) collective-permute-start(f32[16,8,128]{2,1,0:T(8,128)S(1)} %get-tuple-element.22.carried), channel_id=1, source_target_pairs={{0,8},{4,12},{8,16},{12,20},{16,24},{20,28},{24,32},{28,36},{32,40... | collective-permute-start | bytes 196616 | tf_op jit(solution)/shard_map/ppermute | solution.py:302
  32.6 3.6 %collective-permute-start.3 = (f32[16,8,128]{2,1,0:T(8,128)S(1)}, f32[16,8,128]{2,1,0:T(8,128)S(1)}, u32[]{:S(2)}, u32[]{:S(2)}) collective-permute-start(f32[16,8,128]{2,1,0:T(8,128)S(1)} %get-tuple-element.20), channel_id=1, source_target_pairs={{0,64},{4,68},{8,72},{12,76},{16,80},{20,84},{24,88},{28,92},{32,9... | collective-permute-start | bytes 196616 | tf_op jit(solution)/shard_map/ppermute | solution.py:302
  36.2 0.0 collective-permute-done.1.sixth
  36.2 0.1 shard_map.70.far
  36.3 0.0 collective-permute-done.2.fourth
  36.3 0.1 shard_map.71.near
  36.5 0.0 collective-permute-done.4.last
  36.5 2.3 %collective-permute-done.5.ahead = f32[16,8,128]{2,1,0:T(8,128)S(1)} collective-permute-done((f32[16,8,128]{2,1,0:T(8,128)S(1)}, f32[16,8,128]{2,1,0:T(8,128)S(1)}, u32[]{:S(2)}, u32[]{:S(2)}) %collective-permute-start.5) | collective-permute-done | bytes 65568 | tf_op jit(solution)/shard_map/ppermute | solution.py:302
  38.8 2.1 %collective-permute-done.3.second = f32[16,8,128]{2,1,0:T(8,128)S(1)} collective-permute-done((f32[16,8,128]{2,1,0:T(8,128)S(1)}, f32[16,8,128]{2,1,0:T(8,128)S(1)}, u32[]{:S(2)}, u32[]{:S(2)}) %collective-permute-start.3) | collective-permute-done | bytes 65568 | tf_op jit(solution)/shard_map/ppermute | solution.py:302
  40.9 5.5 %shard_map.72 = (f32[8,16,8,128]{3,2,1,0:T(8,128)S(1)}, f32[16,8,128]{2,1,0:T(8,128)S(1)}) custom-call(f32[16,8,128]{2,1,0:T(8,128)S(1)} %shard_map.71.near, f32[16,8,128]{2,1,0:T(8,128)S(1)} %collective-permute-done.3.second, f32[16,8,128]{2,1,0:T(8,128)S(1)} %get-tuple-element.21.before, f32[16,8,128]{2,1,0:T(8,128)S(1)} %get-tuple-element.15.forcing, ...), custom_call_target="tpu_custom_call" | custom-call | flops 50000000 | bytes 3866624 | tf_op jit(solution)/shard_map/pallas_call | solution.py:287
  46.4 14.3 %all_to_all.11.sums = f32[8,16,8,128]{3,2,1,0:T(8,128)S(1)} all-to-all(f32[8,16,8,128]{3,2,1,0:T(8,128)S(1)} %get-tuple-element.23), channel_id=1, replica_groups=mesh['z'=8,'place'=8,'space'=4] {'place'}, dimensions={0} | all-to-all | bytes 1048576 | tf_op jit(solution)/shard_map/all_to_all | solution.py:328
  60.7 0.0 copy-start.1
  60.7 4.4 %shard_map.73 = (f32[96,128]{1,0:T(8,128)S(1)}, f32[96,128]{1,0:T(8,128)S(1)}) custom-call(f32[8,16,8,128]{3,2,1,0:T(8,128)S(1)} %all_to_all.11.sums, f32[16,8,128]{2,1,0:T(8,128)S(1)} %get-tuple-element.24.gap, f32[16,8,128]{2,1,0:T(8,128)S(1)} %get-tuple-element.22.carried, f32[13,16,8,128]{3,2,1,0:T(8,128)S(1)} %get-tuple-element.16.fine2, ...), custom_call_target="tpu_custom_call" | custom-call | flops 30000000 | bytes 4096000 | tf_op jit(solution)/shard_map/pallas_call | solution.py:287
  65.1 0.7 collective-permute-start.6
  65.8 3.5 %collective-permute-done.6.got = f32[96,128]{1,0:T(8,128)S(1)} collective-permute-done((f32[96,128]{1,0:T(8,128)S(1)}, f32[96,128]{1,0:T(8,128)S(1)}, u32[]{:S(2)}, u32[]{:S(2)}) %collective-permute-start.6) | collective-permute-done | bytes 49184 | tf_op jit(solution)/shard_map/ppermute | solution.py:336
  69.3 0.0 copy-done.1
  69.3 0.8 %shard_map.74 = (f32[1,2,16,256]{3,2,1,0:T(8,128)}, f32[1,2,16,256]{3,2,1,0:T(8,128)}, f32[1,2,16,256]{3,2,1,0:T(8,128)}) custom-call(f32[96,128]{1,0:T(8,128)S(1)} %collective-permute-done.6.got, f32[96,128]{1,0:T(8,128)S(1)} %get-tuple-element.26.kept, f32[1,2,16,256]{3,2,1,0:T(8,128)S(1)} %copy-done.1), custom_call_target="tpu_custom_call" | custom-call | flops 10000000 | bytes 229376 | tf_op jit(solution)/shard_map/pallas_call | solution.py:287
Async XLA Ops:
  0.6 0.8 %copy-start = (f32[1,2,16,256]{3,2,1,0:T(8,128)S(1)}, f32[1,2,16,256]{3,2,1,0:T(8,128)}, u32[]{:S(2)}) copy-start(f32[1,2,16,256]{3,2,1,0:T(8,128)} %states.3) | copy-start | bytes 98308
  11.5 6.5 %collective-permute-start = (f32[128,128]{1,0:T(8,128)S(1)}, f32[128,128]{1,0:T(8,128)S(1)}, u32[]{:S(2)}, u32[]{:S(2)}) collective-permute-start(f32[128,128]{1,0:T(8,128)S(1)} %bitcast.4), channel_id=1, source_target_pairs={{0,32},{4,36},{8,40},{12,44},{16,48},{20,52},{24,56},{28,60},{32,6... | collective-permute-start | bytes 196616 | tf_op jit(solution)/shard_map/ppermute | solution.py:302
  21.7 14.5 %collective-permute-start.1 = (f32[16,8,128]{2,1,0:T(8,128)S(1)}, f32[16,8,128]{2,1,0:T(8,128)S(1)}, u32[]{:S(2)}, u32[]{:S(2)}) collective-permute-start(f32[16,8,128]{2,1,0:T(8,128)S(1)} %get-tuple-element.20), channel_id=1, source_target_pairs={{0,192},{4,196},{8,200},{12,204},{16,208},{20,212},{24,216},{28,22... | collective-permute-start | bytes 196616 | tf_op jit(solution)/shard_map/ppermute | solution.py:302
  22.4 14.0 %collective-permute-start.2 = (f32[16,8,128]{2,1,0:T(8,128)S(1)}, f32[16,8,128]{2,1,0:T(8,128)S(1)}, u32[]{:S(2)}, u32[]{:S(2)}) collective-permute-start(f32[16,8,128]{2,1,0:T(8,128)S(1)} %get-tuple-element.20), channel_id=1, source_target_pairs={{0,128},{4,132},{8,136},{12,140},{16,144},{20,148},{24,152},{28,15... | collective-permute-start | bytes 196616 | tf_op jit(solution)/shard_map/ppermute | solution.py:302
  27.2 9.2 %collective-permute-start.4 = (f32[128,128]{1,0:T(8,128)S(1)}, f32[128,128]{1,0:T(8,128)S(1)}, u32[]{:S(2)}, u32[]{:S(2)}) collective-permute-start(f32[128,128]{1,0:T(8,128)S(1)} %bitcast.6), channel_id=1, source_target_pairs={{0,4},{4,8},{8,12},{12,16},{16,20},{20,24},{24,28},{28,32},{32,36}... | collective-permute-start | bytes 196616 | tf_op jit(solution)/shard_map/ppermute | solution.py:302
  29.2 9.6 %collective-permute-start.5 = (f32[16,8,128]{2,1,0:T(8,128)S(1)}, f32[16,8,128]{2,1,0:T(8,128)S(1)}, u32[]{:S(2)}, u32[]{:S(2)}) collective-permute-start(f32[16,8,128]{2,1,0:T(8,128)S(1)} %get-tuple-element.22.carried), channel_id=1, source_target_pairs={{0,8},{4,12},{8,16},{12,20},{16,24},{20,28},{24,32},{28,36},{32,40... | collective-permute-start | bytes 196616 | tf_op jit(solution)/shard_map/ppermute | solution.py:302
  32.6 8.3 %collective-permute-start.3 = (f32[16,8,128]{2,1,0:T(8,128)S(1)}, f32[16,8,128]{2,1,0:T(8,128)S(1)}, u32[]{:S(2)}, u32[]{:S(2)}) collective-permute-start(f32[16,8,128]{2,1,0:T(8,128)S(1)} %get-tuple-element.20), channel_id=1, source_target_pairs={{0,64},{4,68},{8,72},{12,76},{16,80},{20,84},{24,88},{28,92},{32,9... | collective-permute-start | bytes 196616 | tf_op jit(solution)/shard_map/ppermute | solution.py:302
  60.7 8.6 %copy-start.1 = (f32[1,2,16,256]{3,2,1,0:T(8,128)S(1)}, f32[1,2,16,256]{3,2,1,0:T(8,128)}, u32[]{:S(2)}) copy-start(f32[1,2,16,256]{3,2,1,0:T(8,128)} %states.3) | copy-start | bytes 98308
  65.1 4.2 %collective-permute-start.6 = (f32[96,128]{1,0:T(8,128)S(1)}, f32[96,128]{1,0:T(8,128)S(1)}, u32[]{:S(2)}, u32[]{:S(2)}) collective-permute-start(f32[96,128]{1,0:T(8,128)S(1)} %get-tuple-element.25), channel_id=1, source_target_pairs={{0,1},{1,0},{2,3},{3,2},{4,5},{5,4},{6,7},{7,6},{8,9},{9,8},{10,11... | collective-permute-start | bytes 147464 | tf_op jit(solution)/shard_map/ppermute | solution.py:336
